TPU v7x, 128 devices: a whole 4x4x4 slice. The times are simulated.
128 devices in a mesh: dp: 4 (over x), expert: 32 (over z, y, core).
Axes of the slice: x: 4, y: 4, z: 4, core: 2. Of those that a mesh axis runs over, the one named last changes fastest.
Arguments:
- tokens: bfloat16 [32768, 2048], P(('dp', 'expert')), may hold values from -6 to 6
- out_grad: bfloat16 [32768, 2048], P(('dp', 'expert')), may hold values from -6 to 6
- picks: int32 [4, 32, 128], P('dp', 'expert'), may hold values from 0 to 8191, as said below
- gates: float32 [4, 32, 128], P('dp', 'expert'), may hold values from 0.1 to 1
- w_in: bfloat16 [32, 2048, 4096], P('expert', None, 'dp'), may hold values from -0.125 to 0.125
- w_out: bfloat16 [32, 4096, 2048], P('expert', 'dp'), may hold values from -0.09375 to 0.09375
Outputs:
- moe_out: bfloat16 [32768, 2048], P(('dp', 'expert'))
- tokens_grad: bfloat16 [32768, 2048], P(('dp', 'expert'))
- w_in_grad: bfloat16 [32, 2048, 4096], P('expert', None, 'dp')
- w_out_grad: bfloat16 [32, 4096, 2048], P('expert', 'dp')
Inputs may be any that keep to these rules, and one draw needn't show every extreme that they name: Indices of tokens within one group; the 128 picks of one expert in one group are distinct; among the tokens of one device (an aligned block of 256) an expert picks at most 8, and this is reached in every draw.
All inputs are finite; a program needn't handle non-finite values.
Results may differ from a plain program's by a relative error of at most 0.015.
Values may be sent and summed in bfloat16 or wider, within the bound.
No kernel may reach another device: no remote copies, remote signals or barrier semaphores. Data moves between devices by JAX's collectives and lax.ppermute only.
A program may use at most 128 MiB of HBM per device.

v0:
```python
import jax
import jax.numpy as jnp
from jax import lax
from jax.sharding import PartitionSpec as P


def compact_rows(list_picks, tok_dev, slot_size):
    source = list_picks // tok_dev
    picks_total = list_picks.shape[0]
    positions = jnp.arange(picks_total, dtype=jnp.int32)
    earlier = (source[None, :] == source[:, None]) & (positions[None, :] < positions[:, None])
    slot_rank = jnp.sum(earlier.astype(jnp.int32), axis=1)
    return source * slot_size + slot_rank


def on_device(tokens, out_grad, picks, gates, w_in, w_out):
    expert_count = lax.axis_size("expert")
    group_count = lax.axis_size("dp")
    device_index = lax.axis_index("expert")
    tok_dev, width = tokens.shape
    capacity = picks.shape[2]
    slot_size = 2 * capacity // expert_count
    group_picks = lax.all_gather(picks, "expert", axis=1, tiled=True)[0]
    source = group_picks // tok_dev
    position = group_picks % tok_dev
    is_mine = source == device_index
    slot_rank = jnp.cumsum(is_mine.astype(jnp.int32), axis=1) - 1
    slot_ids = jnp.arange(slot_size, dtype=jnp.int32)
    select = (is_mine[:, :, None] & (slot_rank[:, :, None] == slot_ids[None, None, :])).astype(
        jnp.bfloat16
    )
    where_token = (
        position[:, :, None] == jnp.arange(tok_dev, dtype=jnp.int32)[None, None, :]
    ).astype(jnp.bfloat16)
    layout = jnp.einsum(
        "ecs,ect->est", select, where_token, preferred_element_type=jnp.float32
    ).astype(jnp.bfloat16)
    joined = jnp.concatenate([tokens, out_grad], axis=1)
    packed = jnp.einsum("est,td->esd", layout, joined, preferred_element_type=jnp.float32).astype(
        jnp.bfloat16
    )
    own_picks = picks[0, 0]
    own_rows = compact_rows(own_picks, tok_dev, slot_size)
    spread = jnp.broadcast_to(packed[None], (group_count,) + packed.shape)
    spread = spread.reshape(group_count * expert_count, slot_size, 2 * width)
    arrived = lax.all_to_all(spread, ("dp", "expert"), split_axis=0, concat_axis=0, tiled=True)
    arrived = arrived.reshape(group_count, expert_count * slot_size, 2 * width)
    far_picks = lax.all_gather(picks, "dp", axis=0, tiled=True)[:, 0, :]
    index_rows = jax.vmap(lambda lists: compact_rows(lists, tok_dev, slot_size))(far_picks)
    gathered = jnp.take_along_axis(arrived, index_rows[:, :, None], axis=1)
    gathered = gathered.reshape(group_count * capacity, 2 * width)
    row_inputs = gathered[:, :width]
    row_cotangents = gathered[:, width:]
    all_gates = lax.all_gather(gates[:, 0, :], "dp", axis=0, tiled=True).reshape(-1)
    own_gates = gates[0, 0]
    weight_in = w_in[0]
    weight_out = w_out[0]

    def split_sum(matrix_left, matrix_right, contract):
        product = lax.dot_general(
            matrix_left,
            matrix_right,
            (((1,), (contract,)), ((), ())),
            preferred_element_type=jnp.float32,
        )
        return lax.psum_scatter(
            lax.optimization_barrier(product.astype(jnp.bfloat16))
            .astype(jnp.float32)
            .astype(jnp.bfloat16),
            "dp",
            scatter_dimension=0,
            tiled=True,
        ).astype(jnp.float32)

    act = jnp.dot(row_inputs, weight_in, preferred_element_type=jnp.float32)
    hidden, gelu_back = jax.vjp(jax.nn.gelu, act)
    hidden = hidden.astype(jnp.bfloat16)
    summed = split_sum(hidden, weight_out, 0)
    outputs = (own_gates[:, None] * summed).astype(jnp.bfloat16)
    dout = (all_gates[:, None] * row_cotangents.astype(jnp.float32)).astype(jnp.bfloat16)
    dhid = lax.dot_general(
        dout, weight_out, (((1,), (1,)), ((), ())), preferred_element_type=jnp.float32
    )
    dact = gelu_back(dhid)[0].astype(jnp.bfloat16)
    dinput = split_sum(dact, weight_in, 1).astype(jnp.bfloat16)
    grad_in = lax.dot_general(
        row_inputs, dact, (((0,), (0,)), ((), ())), preferred_element_type=jnp.float32
    ).astype(jnp.bfloat16)
    grad_out = lax.dot_general(
        hidden, dout, (((0,), (0,)), ((), ())), preferred_element_type=jnp.float32
    ).astype(jnp.bfloat16)
    returning = jnp.concatenate([outputs, dinput], axis=1)
    place_back = (
        own_rows[:, None] == jnp.arange(expert_count * slot_size, dtype=jnp.int32)[None, :]
    ).astype(jnp.bfloat16)
    outgoing = jnp.einsum(
        "cr,cd->rd", place_back, returning, preferred_element_type=jnp.float32
    ).astype(jnp.bfloat16)
    outgoing = outgoing.reshape(expert_count, slot_size, 2 * width)
    came_back = lax.all_to_all(outgoing, "expert", split_axis=0, concat_axis=0, tiled=True)
    totals = jnp.einsum("est,esd->td", layout, came_back, preferred_element_type=jnp.float32)
    moe_out = totals[:, :width].astype(jnp.bfloat16)
    tokens_grad = totals[:, width:].astype(jnp.bfloat16)
    return (moe_out, tokens_grad, grad_in[None], grad_out[None])


def solution(mesh):
    return jax.shard_map(
        on_device,
        mesh=mesh,
        in_specs=(
            P(("dp", "expert"), None),
            P(("dp", "expert"), None),
            P("dp", "expert", None),
            P("dp", "expert", None),
            P("expert", None, "dp"),
            P("expert", "dp", None),
        ),
        out_specs=(
            P(("dp", "expert"), None),
            P(("dp", "expert"), None),
            P("expert", None, "dp"),
            P("expert", "dp", None),
        ),
        check_vma=False,
    )
```

profile of v0, /device:TPU:1, one launch (start us, length us, event | category | flops | bytes accessed | tf_op | source)
XLA Modules:
  0.0 292.9 jit_solution(13818033031015786607)
XLA Ops:
  7.2 24.3 %all_gather.9 = s32[1,32,128]{2,0,1:T(1,128)S(1)} all-gather(s32[1,1,128]{2,0,1:T(1,128)} %bitcast.72), channel_id=1, replica_groups=mesh['dp'=4,'expert'=32] {'expert'}, dimensions={1}, use_global_device_ids=true | all-gather | bytes 16896 | tf_op jit(solution)/shard_map/all_gather | solution.py:23
  31.4 0.3 reduce_window_sum.11
  31.7 1.0 fusion.31
  32.8 2.3 convolution_convert_fusion.1
  35.0 4.3 %broadcast_in_dim.13 = bf16[4,32,8,4096]{3,2,1,0:T(8,128)(2,1)} broadcast(bf16[32,8,4096]{2,1,0:T(8,128)(2,1)S(1)} %convolution_convert_fusion.1), dimensions={1,2,3} | broadcast | bytes 10485760 | tf_op jit(solution)/shard_map/broadcast_in_dim | solution.py:44
  39.3 0.0 copy-start.3
  39.3 7.8 %all-to-all-start = ((bf16[128,8,4096]{2,1,0:T(8,128)(2,1)}), bf16[128,8,4096]{2,1,0:T(8,128)(2,1)}, u32[]{:S(2)}, u32[]{:S(2)}) async-start(bf16[128,8,4096]{2,1,0:T(8,128)(2,1)} %bitcast.64), calls=%async_computation | async-start | bytes 16777216 | tf_op jit(solution)/shard_map/all_to_all | solution.py:46
  47.1 0.0 reduce-scatter.3.cloned.1.call-start
  47.2 0.0 copy-done.3
  47.2 106.0 %all_gather.10 = s32[4,1,128]{2,1,0:T(1,128)S(1)} all-gather(s32[1,1,128]{2,1,0:T(1,128)S(1)} %copy-done.3), channel_id=1, replica_groups=mesh['dp'=4,'expert'=32] {'dp'}, dimensions={0}, use_global_device_ids=true | all-gather | bytes 2560 | tf_op jit(solution)/shard_map/all_gather | solution.py:48
  153.3 0.2 convert_reduce_fusion
  153.5 0.0 all-to-all-done
  153.6 17.3 %gather_fusion = bf16[512,4096]{1,0:T(8,128)(2,1)} fusion(bf16[4,256,4096]{2,1,0:T(8,128)(2,1)} %bitcast.10, s32[512]{0:T(512)S(1)} %or_bitcast_fusion), kind=kCustom, calls=%fused_computation | custom fusion | bytes 8392704 | tf_op jit(solution)/shard_map/jit(take_along_axis)/gather | solution.py:50
  170.9 0.0 copy-start.5
  170.9 2.8 broadcast_select_fusion
  173.6 0.7 copy-done.5
  174.3 0.0 copy-start
  174.3 0.0 copy-start.4
  174.3 2.3 fusion.8
  176.7 0.0 copy-done
  176.7 0.0 copy-start.7
  176.7 1.3 copy-done.7
  178.0 0.7 copy-done.4
  178.8 3.8 %fusion.14 = bf16[512,2048]{1,0:T(8,128)(2,1)} fusion(bf16[1,1024,2048]{2,1,0:T(8,128)(2,1)S(1)} %copy-done.4, f32[512,1024]{1,0:T(8,128)S(1)} %fusion.8), kind=kOutput, calls=%fused_computation.23 | convolution fusion | flops 2153250816 | bytes 8388608 | tf_op jit(solution)/shard_map/dot_general | solution.py:60
  182.6 0.0 copy-start.2
  182.6 0.0 reduce-scatter.3.cloned.1.call-update
  182.6 0.0 reduce-scatter.5.cloned.1.call-start
  182.7 0.6 copy-done.2
  183.3 6.1 %all-gather = f32[4,1,128]{2,1,0:T(1,128)S(1)} all-gather(f32[1,1,128]{2,1,0:T(1,128)S(1)} %copy-done.2), channel_id=2, replica_groups=mesh['dp'=4,'expert'=32] {'dp'}, dimensions={0}, use_global_device_ids=true | all-gather | bytes 2560 | tf_op jit(solution)/shard_map/all_gather | solution.py:54
  189.4 7.4 %fusion.23 = bf16[512,1024]{1,0:T(8,128)(2,1)S(1)} fusion(f32[512,1024]{1,0:T(8,128)} %copy-done.7, bf16[1,1024,2048]{2,1,0:T(8,128)(2,1)} %param.11, bf16[512,4096]{1,0:T(8,128)(2,1)} %copy-done, f32[512]{0:T(512)S(1)} %bitcast.73), kind=kOutput, calls=%fused_computation.30 | convolution fusion | flops 2161115136 | bytes 9439232 | tf_op jit(solution)/shard_map/dot_general | solution.py:81
  196.8 0.0 copy-done.6
  196.8 3.7 %fusion.11 = bf16[512,2048]{1,0:T(8,128)(2,1)} fusion(bf16[512,1024]{1,0:T(8,128)(2,1)S(1)} %fusion.23, bf16[1,2048,1024]{2,1,0:T(8,128)(2,1)S(1)} %copy-done.6), kind=kOutput, calls=%fused_computation.22 | convolution fusion | flops 2148532224 | bytes 7340032 | tf_op jit(solution)/shard_map/dot_general | solution.py:60
  200.5 0.0 reduce-scatter.5.cloned.1.call-update
  200.6 0.2 convert_reduce_fusion.1
  200.8 12.0 %reduce-scatter.3.cloned.1.call-done = bf16[128,2048]{1,0:T(8,128)(2,1)} async-done(((bf16[512,2048]{1,0:T(8,128)(2,1)}), bf16[128,2048]{1,0:T(8,128)(2,1)}) %reduce-scatter.3.cloned.1.call-update) | async-done | bytes 524304 | tf_op jit(solution)/shard_map/reduce_scatter | solution.py:66
  212.8 1.2 multiply_convert_fusion.2
  214.0 31.3 %reduce-scatter.5.cloned.1.call-done = bf16[128,2048]{1,0:T(8,128)(2,1)} async-done(((bf16[512,2048]{1,0:T(8,128)(2,1)}), bf16[128,2048]{1,0:T(8,128)(2,1)}) %reduce-scatter.5.cloned.1.call-update) | async-done | bytes 524304 | tf_op jit(solution)/shard_map/reduce_scatter | solution.py:66
  245.3 3.2 %fusion.1 = bf16[32,8,4096]{2,1,0:T(8,128)(2,1)} fusion(bf16[128,2048]{1,0:T(8,128)(2,1)} %reduce-scatter.5.cloned.1.call-done, bf16[128,2048]{1,0:T(8,128)(2,1)S(1)} %multiply_convert_fusion.2, s32[128]{0:T(128)S(1)} %multiply_add_fusion), kind=kOutput, calls=%fused_computation.5 | convolution fusion | flops 271613952 | bytes 3146240 | tf_op jit(solution)/shard_map/cr,cd->rd/dot_general | solution.py:96
  248.4 7.7 %all-to-all-start.1 = ((bf16[32,8,4096]{2,1,0:T(8,128)(2,1)}), bf16[32,8,4096]{2,1,0:T(8,128)(2,1)S(1)}, u32[]{:S(2)}, u32[]{:S(2)}) async-start(bf16[32,8,4096]{2,1,0:T(8,128)(2,1)} %fusion.1), calls=%async_computation.3 | async-start | bytes 4194304 | tf_op jit(solution)/shard_map/all_to_all | solution.py:100
  256.1 0.0 copy-start.1
  256.1 0.0 copy-start.8
  256.1 6.1 %convert_bitcast_fusion.1 = bf16[1,2048,1024]{2,1,0:T(8,128)(2,1)} fusion(bf16[512,1024]{1,0:T(8,128)(2,1)S(1)} %fusion.23, bf16[512,4096]{1,0:T(8,128)(2,1)} %copy-done), kind=kOutput, calls=%fused_computation.15 | convolution fusion | flops 2149580800 | bytes 7340032 | tf_op jit(solution)/shard_map/dot_general | solution.py:86
  262.3 0.0 copy-done.1
  262.3 0.0 copy-done.8
  262.3 4.8 %convert_bitcast_fusion = bf16[1,1024,2048]{2,1,0:T(8,128)(2,1)} fusion(bf16[512,4096]{1,0:T(8,128)(2,1)S(1)} %copy-done.1, f32[512]{0:T(512)S(1)} %bitcast.74, f32[512,1024]{1,0:T(8,128)S(1)} %copy-done.8), kind=kOutput, calls=%fused_computation.14 | convolution fusion | flops 2157445120 | bytes 8390656 | tf_op jit(solution)/shard_map/dot_general | solution.py:89
  267.1 16.7 %all-to-all-done.1 = bf16[32,8,4096]{2,1,0:T(8,128)(2,1)S(1)} async-done(((bf16[32,8,4096]{2,1,0:T(8,128)(2,1)}), bf16[32,8,4096]{2,1,0:T(8,128)(2,1)S(1)}, u32[]{:S(2)}, u32[]{:S(2)}) %all-to-all-start.1) | async-done | bytes 2097184 | tf_op jit(solution)/shard_map/all_to_all | solution.py:100
  283.9 0.8 fusion
  284.6 1.5 fusion.57
  (10 shorter events, 0.1 us)
Async XLA Ops:
  39.3 7.9 %copy-start.3 = (s32[1,1,128]{2,1,0:T(1,128)S(1)}, s32[1,1,128]{2,1,0:T(1,128)}, u32[]{:S(2)}) copy-start(s32[1,1,128]{2,1,0:T(1,128)} %param.8) | copy-start | bytes 1540
  39.3 114.3 %all-to-all-start = ((bf16[128,8,4096]{2,1,0:T(8,128)(2,1)}), bf16[128,8,4096]{2,1,0:T(8,128)(2,1)}, u32[]{:S(2)}, u32[]{:S(2)}) async-start(bf16[128,8,4096]{2,1,0:T(8,128)(2,1)} %bitcast.64), calls=%async_computation | async-start | bytes 16777216 | tf_op jit(solution)/shard_map/all_to_all | solution.py:46
  47.1 165.6 %reduce-scatter.3.cloned.1.call-start = ((), (), s32[]{:S(2)}) async-start(), calls=%async_computation.4 | async-start | bytes 2621440 | tf_op jit(solution)/shard_map/reduce_scatter | solution.py:66
  170.9 3.4 %copy-start.5 = (bf16[1,2048,1024]{2,1,0:T(8,128)(2,1)S(1)}, bf16[1,2048,1024]{2,1,0:T(8,128)(2,1)}, u32[]{:S(2)}) copy-start(bf16[1,2048,1024]{2,1,0:T(8,128)(2,1)} %param.10) | copy-start | bytes 12582916
  174.3 2.4 copy-start
  174.3 4.5 %copy-start.4 = (bf16[1,1024,2048]{2,1,0:T(8,128)(2,1)S(1)}, bf16[1,1024,2048]{2,1,0:T(8,128)(2,1)}, u32[]{:S(2)}) copy-start(bf16[1,1024,2048]{2,1,0:T(8,128)(2,1)} %param.11) | copy-start | bytes 12582916
  176.7 1.3 copy-start.7
  182.6 0.7 copy-start.2
  182.6 62.6 %reduce-scatter.5.cloned.1.call-start = ((), (), s32[]{:S(2)}) async-start(), calls=%async_computation.5 | async-start | bytes 2621440 | tf_op jit(solution)/shard_map/reduce_scatter | solution.py:66
  189.4 7.4 %copy-start.6 = (bf16[1,2048,1024]{2,1,0:T(8,128)(2,1)S(1)}, bf16[1,2048,1024]{2,1,0:T(8,128)(2,1)}, u32[]{:S(2)}) copy-start(bf16[1,2048,1024]{2,1,0:T(8,128)(2,1)} %param.10) | copy-start | bytes 12582916
  248.4 35.4 %all-to-all-start.1 = ((bf16[32,8,4096]{2,1,0:T(8,128)(2,1)}), bf16[32,8,4096]{2,1,0:T(8,128)(2,1)S(1)}, u32[]{:S(2)}, u32[]{:S(2)}) async-start(bf16[32,8,4096]{2,1,0:T(8,128)(2,1)} %fusion.1), calls=%async_computation.3 | async-start | bytes 4194304 | tf_op jit(solution)/shard_map/all_to_all | solution.py:100
  256.1 6.2 %copy-start.1 = (bf16[512,4096]{1,0:T(8,128)(2,1)S(1)}, bf16[512,4096]{1,0:T(8,128)(2,1)}, u32[]{:S(2)}) copy-start(bf16[512,4096]{1,0:T(8,128)(2,1)} %copy-done) | copy-start | bytes 12582916
  256.1 6.2 %copy-start.8 = (f32[512,1024]{1,0:T(8,128)S(1)}, f32[512,1024]{1,0:T(8,128)}, u32[]{:S(2)}) copy-start(f32[512,1024]{1,0:T(8,128)} %copy-done.7) | copy-start | bytes 6291460
Sparse Core Ops, SparseCore 0:
  182.8 29.9 reduce-scatter.2
  215.9 29.3 reduce-scatter.4
where the time goes:
time: 295 us; the launch traced here: 293 us
  blocking collectives  136 us (46%)
  waiting for transfers between devices  60.1 us (20%)
  matrix products  35.5 us (12%)
  local copies, waits for them, and re-layouts  26.4 us (9%)
  starting transfers between devices  15.6 us (5%)
  between operations  14.2 us (5%)
  other arithmetic  4.79 us (2%)
    all_gather x1, blocking collectives, on_device(): far_picks = lax.all_gather(picks, 'dp', axis=0, tiled=True)[:, 0, :]  106 us
    reduce_scatter x2, waiting for transfers between devices, split_sum(): lax.psum_scatter(lax.optimization_barrier(product.astype(jnp.bfloat16)).a...  43.3 us
    all_gather x1, blocking collectives, on_device(): group_picks = lax.all_gather(picks, 'expert', axis=1, tiled=True)[0]  24.3 us
    gather x1, local copies, waits for them, and re-layouts, on_device(): gathered = jnp.take_along_axis(arrived, index_rows[:, :, None], axis=1)  17.3 us
    all_to_all x1, waiting for transfers between devices, on_device(): lax.all_to_all(outgoing, 'expert', split_axis=0, concat_axis=0, tiled=True)  16.7 us
    all_to_all x1, starting transfers between devices, on_device(): lax.all_to_all(spread, ('dp', 'expert'), split_axis=0, concat_axis=0, til...  7.83 us
    all_to_all x1, starting transfers between devices, on_device(): lax.all_to_all(outgoing, 'expert', split_axis=0, concat_axis=0, tiled=True)  7.66 us
    dot_general x2, matrix products, split_sum(): lax.dot_general(matrix_left, matrix_right, (((1,), (contract,)), ((), ())...  7.54 us
  transfers between devices with their start and end apart: 4, of which 3 were waited for; matrix products, arithmetic and copies ran while one was open for 8% of the time, Pallas kernels for 0%

commit v1 on v0

v1 whole, which is shorter than its diff:
```python
import jax
import jax.numpy as jnp
from jax import lax
from jax.sharding import PartitionSpec as P

F32 = jnp.float32
BF16 = jnp.bfloat16


def shifted(array, step):
    count = lax.axis_size("dp")
    return lax.ppermute(array, "dp", [(i, (i + step) % count) for i in range(count)])


def ring_gather(own):
    half = own.shape[0] // 2
    below = shifted(own, 1)
    above = shifted(own, -1)
    far_upper = shifted(below[:half], 1)
    far_lower = shifted(above[half:], -1)
    return own, below, above, far_upper, far_lower


def ring_sum(parts):
    own, below, above, far = jnp.split(parts, 4, axis=0)
    half = own.shape[0] // 2
    far = far.astype(BF16)
    to_above = shifted(far[:half], 1)
    to_below = shifted(far[half:], -1)
    above = jnp.concatenate(
        [(above[:half] + to_above.astype(F32)).astype(BF16), above[half:].astype(BF16)], axis=0
    )
    below = jnp.concatenate(
        [below[:half].astype(BF16), (below[half:] + to_below.astype(F32)).astype(BF16)], axis=0
    )
    from_below = shifted(above, 1)
    from_above = shifted(below, -1)
    return own + from_below.astype(F32) + from_above.astype(F32)


def swap(array):
    return lax.all_to_all(array, "expert", split_axis=0, concat_axis=0, tiled=True)


def on_device(tokens, out_grad, picks, gates, w_in, w_out):
    experts = lax.axis_size("expert")
    tok_dev, width = tokens.shape
    capacity = picks.shape[2]
    slot_size = 2 * capacity // experts
    slots = experts * slot_size

    own_picks = picks[0, 0]
    source = own_picks // tok_dev
    order = jnp.arange(capacity, dtype=jnp.int32)
    earlier = (source[None, :] == source[:, None]) & (order[None, :] < order[:, None])
    rank = jnp.sum(earlier.astype(jnp.int32), axis=1)
    slot_of = source * slot_size + rank
    place = slot_of[None, :] == jnp.arange(slots, dtype=jnp.int32)[:, None]
    wanted = jnp.sum(jnp.where(place, own_picks[None, :] % tok_dev + 1, 0), axis=1)
    wanted = jnp.broadcast_to(wanted.astype(F32)[:, None], (slots, 128))
    place = place.astype(BF16)

    asked = swap(wanted.reshape(experts, slot_size, 128)).reshape(slots, 128)[:, :1]
    layout = (
        asked.astype(jnp.int32) == jnp.arange(1, tok_dev + 1, dtype=jnp.int32)[None, :]
    ).astype(BF16)

    def send(rows):
        packed = jnp.dot(layout, rows, preferred_element_type=F32).astype(BF16)
        return swap(packed.reshape(experts, slot_size, width)).reshape(slots, width)

    def unslot(rows):
        return lax.dot_general(place, rows, (((0,), (0,)), ((), ())), preferred_element_type=F32)

    def back(rows):
        placed = jnp.dot(place, rows, preferred_element_type=F32).astype(BF16)
        came = swap(placed.reshape(experts, slot_size, width)).reshape(slots, width)
        return lax.dot_general(
            layout, came, (((0,), (0,)), ((), ())), preferred_element_type=F32
        ).astype(BF16)

    own_gates = gates[0, 0][:, None]
    weight_in = w_in[0]
    weight_out = w_out[0]

    came_in = send(tokens)
    came_in, out_grad = lax.optimization_barrier((came_in, out_grad))
    came_cot = send(out_grad)
    inputs = ring_gather(unslot(came_in).astype(BF16))
    dout_own = (own_gates * unslot(came_cot)).astype(BF16)
    dout_own, inputs = lax.optimization_barrier((dout_own, inputs))
    dout = ring_gather(dout_own)
    inputs = jnp.concatenate(inputs, axis=0)
    dout = jnp.concatenate(dout, axis=0)

    act = jnp.dot(inputs, weight_in, preferred_element_type=F32)
    hidden, gelu_back = jax.vjp(jax.nn.gelu, act)
    hidden = hidden.astype(BF16)
    part = jnp.dot(hidden, weight_out, preferred_element_type=F32)
    summed = ring_sum(part)
    outputs = (own_gates * summed).astype(BF16)

    dhid = lax.dot_general(dout, weight_out, (((1,), (1,)), ((), ())), preferred_element_type=F32)
    dact = gelu_back(dhid)[0].astype(BF16)
    dpart = lax.dot_general(dact, weight_in, (((1,), (1,)), ((), ())), preferred_element_type=F32)
    outputs, dpart = lax.optimization_barrier((outputs, dpart))
    moe_out = back(outputs)
    dinput = ring_sum(dpart).astype(BF16)
    tokens_grad = back(dinput)

    grad_in = lax.dot_general(
        inputs, dact, (((0,), (0,)), ((), ())), preferred_element_type=F32
    ).astype(BF16)
    grad_out = lax.dot_general(
        hidden, dout, (((0,), (0,)), ((), ())), preferred_element_type=F32
    ).astype(BF16)
    return (moe_out, tokens_grad, grad_in[None], grad_out[None])


def solution(mesh):
    return jax.shard_map(
        on_device,
        mesh=mesh,
        in_specs=(
            P(("dp", "expert"), None),
            P(("dp", "expert"), None),
            P("dp", "expert", None),
            P("dp", "expert", None),
            P("expert", None, "dp"),
            P("expert", "dp", None),
        ),
        out_specs=(
            P(("dp", "expert"), None),
            P(("dp", "expert"), None),
            P("expert", None, "dp"),
            P("expert", "dp", None),
        ),
        check_vma=False,
    )
```

time: 295 us -> 187 us (0.63)
  blocking collectives: 136 us -> 20.8 us
  starting transfers between devices: 15.6 us -> 54.1 us
  local copies, waits for them, and re-layouts: 26.4 us -> 9.12 us
  between operations: 14.2 us -> 1.08 us
  waiting for transfers between devices: 60.1 us -> 66.2 us
  matrix products: 35.5 us -> 31.5 us
    all_gather x3 -> x0, blocking collectives: 136 us -> none  [the longest x1 106 us: on_device(): far_picks = lax.all_gather(picks, 'dp', axis=0, tiled=True)[:, 0, :]]
    ppermute x0 -> x16, waiting for transfers between devices: none -> 53.9 us  [shifted(): lax.ppermute(array, 'dp', [(i, (i + step) % count) for i in range(count)])]
    reduce_scatter x2 -> x0, waiting for transfers between devices: 43.3 us -> none  [split_sum(): lax.psum_scatter(lax.optimization_barrier(product.astype(jnp.bfloat16)).a...]
    ppermute x0 -> x16, starting transfers between devices: none -> 21.3 us  [shifted(): lax.ppermute(array, 'dp', [(i, (i + step) % count) for i in range(count)])]
    all_to_all x0 -> x1, blocking collectives: none -> 20.8 us  [swap(): lax.all_to_all(array, 'expert', split_axis=0, concat_axis=0, tiled=True)]
    all_to_all x2 -> x4, starting transfers between devices: 15.5 us -> 32.8 us  [swap(): lax.all_to_all(array, 'expert', split_axis=0, concat_axis=0, tiled=True)]
    gather x1 -> x0, local copies, waits for them, and re-layouts: 17.3 us -> none  [on_device(): gathered = jnp.take_along_axis(arrived, index_rows[:, :, None], axis=1)]
    all_to_all x2 -> x4, waiting for transfers between devices: 16.8 us -> 12.2 us  [swap(): lax.all_to_all(array, 'expert', split_axis=0, concat_axis=0, tiled=True)]
  transfers between devices with their start and end apart: 4 -> 20, of which waited for: 3 -> 9; matrix products, arithmetic and copies ran while one was open for 8% -> 14% of each run, Pallas kernels for 0% -> 0%
where the time goes in v1:
time: 187 us; the launch traced here: 186 us
  waiting for transfers between devices  66.2 us (35%)
  starting transfers between devices  54.1 us (29%)
  matrix products  31.5 us (17%)
  blocking collectives  20.8 us (11%)
  local copies, waits for them, and re-layouts  9.12 us (5%)
  other arithmetic  3.36 us (2%)
    ppermute x16, waiting for transfers between devices, shifted(): lax.ppermute(array, 'dp', [(i, (i + step) % count) for i in range(count)])  53.9 us
    all_to_all x4, starting transfers between devices, swap(): lax.all_to_all(array, 'expert', split_axis=0, concat_axis=0, tiled=True)  32.8 us
    ppermute x16, starting transfers between devices, shifted(): lax.ppermute(array, 'dp', [(i, (i + step) % count) for i in range(count)])  21.3 us
    all_to_all x1, blocking collectives, swap(): lax.all_to_all(array, 'expert', split_axis=0, concat_axis=0, tiled=True)  20.8 us
    all_to_all x4, waiting for transfers between devices, swap(): lax.all_to_all(array, 'expert', split_axis=0, concat_axis=0, tiled=True)  12.2 us
    dot_general x1, matrix products, on_device(): lax.dot_general(inputs, dact, (((0,), (0,)), ((), ())), preferred_element...  6.4 us
    unnamed x33, local copies, waits for them, and re-layouts  5.47 us
    dot_general x1, matrix products, on_device(): lax.dot_general(hidden, dout, (((0,), (0,)), ((), ())), preferred_element...  4.59 us
  transfers between devices with their start and end apart: 20, of which 9 were waited for; matrix products, arithmetic and copies ran while one was open for 14% of the time, Pallas kernels for 0%

profile of v1, /device:TPU:1, one launch (start us, length us, event | category | flops | bytes accessed | tf_op | source)
XLA Modules:
  0.0 186.1 jit_solution(3203628468175296994)
XLA Ops:
  0.6 0.8 and_select_fusion.1
  1.8 0.8 broadcast_in_dim.20
  2.6 9.6 %all-to-all-start = ((f32[32,8,128]{2,1,0:T(8,128)}), f32[32,8,128]{2,1,0:T(8,128)S(1)}, u32[]{:S(2)}, u32[]{:S(2)}) async-start(f32[32,8,128]{2,1,0:T(8,128)} %broadcast_in_dim.20), calls=%async_computation | async-start | bytes 262144 | tf_op jit(solution)/shard_map/all_to_all | solution.py:42
  12.2 7.6 %all-to-all-done = f32[32,8,128]{2,1,0:T(8,128)S(1)} async-done(((f32[32,8,128]{2,1,0:T(8,128)}), f32[32,8,128]{2,1,0:T(8,128)S(1)}, u32[]{:S(2)}, u32[]{:S(2)}) %all-to-all-start) | async-done | bytes 131104 | tf_op jit(solution)/shard_map/all_to_all | solution.py:42
  19.9 0.5 fusion.8
  20.4 20.8 %all_to_all.25 = bf16[32,8,2048]{2,1,0:T(8,128)(2,1)S(1)} all-to-all(bf16[32,8,2048]{2,1,0:T(8,128)(2,1)S(1)} %fusion.8), channel_id=1, replica_groups=mesh['dp'=4,'expert'=32] {'expert'}, dimensions={0} | all-to-all | bytes 2097152 | tf_op jit(solution)/shard_map/all_to_all | solution.py:42
  41.2 1.4 fusion.9
  42.7 4.1 %all-to-all-start.2 = ((bf16[32,8,2048]{2,1,0:T(8,128)(2,1)}), bf16[32,8,2048]{2,1,0:T(8,128)(2,1)S(1)}, u32[]{:S(2)}, u32[]{:S(2)}) async-start(bf16[32,8,2048]{2,1,0:T(8,128)(2,1)} %fusion.9), calls=%async_computation.2 | async-start | bytes 2097152 | tf_op jit(solution)/shard_map/all_to_all | solution.py:42
  47.2 1.3 collective-permute-start
  48.5 1.5 collective-permute-start.1
  49.9 11.7 %collective-permute-done = bf16[128,2048]{1,0:T(8,128)(2,1)S(1)} collective-permute-done((bf16[128,2048]{1,0:T(8,128)(2,1)S(1)}, bf16[128,2048]{1,0:T(8,128)(2,1)S(1)}, u32[]{:S(2)}, u32[]{:S(2)}) %collective-permute-start) | collective-permute-done | bytes 524320 | tf_op jit(solution)/shard_map/ppermute | solution.py:12
  61.6 0.7 slice.85
  62.4 0.7 slice.86
  63.1 2.7 %collective-permute-start.3 = (bf16[64,2048]{1,0:T(8,128)(2,1)}, bf16[64,2048]{1,0:T(8,128)(2,1)}, u32[]{:S(2)}, u32[]{:S(2)}) collective-permute-start(bf16[64,2048]{1,0:T(8,128)(2,1)} %slice.86), channel_id=1, source_target_pairs={{0,96},{32,0},{64,32},{96,64},{1,97},{33,1},{65,33},{97,65},{2,98}... | collective-permute-start | bytes 786440 | tf_op jit(solution)/shard_map/ppermute | solution.py:12
  65.8 0.4 fusion.12
  66.1 4.3 %collective-permute-done.2 = bf16[64,2048]{1,0:T(8,128)(2,1)S(1)} collective-permute-done((bf16[64,2048]{1,0:T(8,128)(2,1)}, bf16[64,2048]{1,0:T(8,128)(2,1)S(1)}, u32[]{:S(2)}, u32[]{:S(2)}) %collective-permute-start.2) | collective-permute-done | bytes 262176 | tf_op jit(solution)/shard_map/ppermute | solution.py:12
  70.4 1.1 constant_dynamic-update-slice_fusion.4
  71.6 1.1 constant_dynamic-update-slice_fusion
  72.8 1.3 copy-done.4
  74.1 2.4 %fusion.6 = f32[512,1024]{1,0:T(8,128)S(1)} fusion(bf16[512,2048]{1,0:T(8,128)(2,1)S(1)} %constant_dynamic-update-slice_fusion, bf16[1,2048,1024]{2,1,0:T(8,128)(2,1)S(1)} %copy-done.9), kind=kOutput, calls=%fused_computation.6 | convolution fusion | flops 2147483648 | bytes 8388608 | tf_op jit(solution)/shard_map/dot_general | solution.py:96
  76.5 2.5 %fusion.51 = (bf16[512,2048]{1,0:T(8,128)(2,1)S(1)}, f32[512,2048]{1,0:T(8,128)S(1)}) fusion(bf16[1,1024,2048]{2,1,0:T(8,128)(2,1)S(1)} %copy-done.8, f32[512,1024]{1,0:T(8,128)S(1)} %fusion.6), kind=kOutput, calls=%fused_computation.95 | convolution fusion | flops 2153250816 | bytes 12582912 | tf_op jit(solution)/shard_map/dot_general | solution.py:99
  79.1 0.6 collective-permute-start.4
  79.8 2.8 %collective-permute-start.6 = (bf16[64,2048]{1,0:T(8,128)(2,1)S(1)}, bf16[64,2048]{1,0:T(8,128)(2,1)S(1)}, u32[]{:S(2)}, u32[]{:S(2)}) collective-permute-start(bf16[64,2048]{1,0:T(8,128)(2,1)S(1)} %get-tuple-element.33), channel_id=1, source_target_pairs={{0,96},{32,0},{64,32},{96,64},{1,97},{33,1},{65,33},{97,65},{2,98}... | collective-permute-start | bytes 786440 | tf_op jit(solution)/shard_map/ppermute | solution.py:12
  82.5 2.7 %collective-permute-start.9 = (bf16[128,2048]{1,0:T(8,128)(2,1)S(1)}, bf16[128,2048]{1,0:T(8,128)(2,1)S(1)}, u32[]{:S(2)}, u32[]{:S(2)}) collective-permute-start(bf16[128,2048]{1,0:T(8,128)(2,1)S(1)} %fusion.12), channel_id=1, source_target_pairs={{0,96},{32,0},{64,32},{96,64},{1,97},{33,1},{65,33},{97,65},{2,98}... | collective-permute-start | bytes 1572872 | tf_op jit(solution)/shard_map/ppermute | solution.py:12
  85.2 1.5 collective-permute-done.4
  86.9 2.3 %collective-permute-start.7 = (bf16[128,2048]{1,0:T(8,128)(2,1)S(1)}, bf16[128,2048]{1,0:T(8,128)(2,1)S(1)}, u32[]{:S(2)}, u32[]{:S(2)}) collective-permute-start(bf16[128,2048]{1,0:T(8,128)(2,1)S(1)} %pad_maximum_fusion.1), channel_id=1, source_target_pairs={{0,96},{32,0},{64,32},{96,64},{1,97},{33,1},{65,33},{97,65},{2,98}... | collective-permute-start | bytes 1572872 | tf_op jit(solution)/shard_map/ppermute | solution.py:12
  89.3 8.6 %collective-permute-done.8 = bf16[128,2048]{1,0:T(8,128)(2,1)S(1)} collective-permute-done((bf16[128,2048]{1,0:T(8,128)(2,1)S(1)}, bf16[128,2048]{1,0:T(8,128)(2,1)S(1)}, u32[]{:S(2)}, u32[]{:S(2)}) %collective-permute-start.8) | collective-permute-done | bytes 524320 | tf_op jit(solution)/shard_map/ppermute | solution.py:12
  98.1 2.9 %collective-permute-start.11 = (bf16[64,2048]{1,0:T(8,128)(2,1)S(1)}, bf16[64,2048]{1,0:T(8,128)(2,1)S(1)}, u32[]{:S(2)}, u32[]{:S(2)}) collective-permute-start(bf16[64,2048]{1,0:T(8,128)(2,1)S(1)} %slice.94), channel_id=1, source_target_pairs={{0,96},{32,0},{64,32},{96,64},{1,97},{33,1},{65,33},{97,65},{2,98}... | collective-permute-start | bytes 786440 | tf_op jit(solution)/shard_map/ppermute | solution.py:12
  101.0 13.7 %collective-permute-done.10 = bf16[64,2048]{1,0:T(8,128)(2,1)S(1)} collective-permute-done((bf16[64,2048]{1,0:T(8,128)(2,1)S(1)}, bf16[64,2048]{1,0:T(8,128)(2,1)S(1)}, u32[]{:S(2)}, u32[]{:S(2)}) %collective-permute-start.10) | collective-permute-done | bytes 262176 | tf_op jit(solution)/shard_map/ppermute | solution.py:12
  114.8 1.4 copy-done.5
  116.2 3.4 %fusion.19 = bf16[512,1024]{1,0:T(8,128)(2,1)S(1)} fusion(f32[512,1024]{1,0:T(8,128)S(1)} %fusion.6, bf16[512,2048]{1,0:T(8,128)(2,1)S(1)} %constant_dynamic-update-slice_fusion.5, bf16[1,1024,2048]{2,1,0:T(8,128)(2,1)S(1)} %copy-done.8), kind=kOutput, calls=%fused_computation.31 | convolution fusion | flops 2157969408 | bytes 9437184 | tf_op jit(solution)/shard_map/dot_general | solution.py:103
  119.7 2.4 %fusion.4 = f32[512,2048]{1,0:T(8,128)S(1)} fusion(bf16[512,1024]{1,0:T(8,128)(2,1)S(1)} %fusion.19, bf16[1,2048,1024]{2,1,0:T(8,128)(2,1)S(1)} %copy-done.9), kind=kOutput, calls=%fused_computation.4 | convolution fusion | flops 2147483648 | bytes 9437184 | tf_op jit(solution)/shard_map/dot_general | solution.py:105
  122.6 1.4 copy-done.1
  124.2 0.6 collective-permute-start.12
  124.8 2.1 %collective-permute-start.14 = (bf16[64,2048]{1,0:T(8,128)(2,1)S(1)}, bf16[64,2048]{1,0:T(8,128)(2,1)}, u32[]{:S(2)}, u32[]{:S(2)}) collective-permute-start(bf16[64,2048]{1,0:T(8,128)(2,1)S(1)} %get-tuple-element.29), channel_id=1, source_target_pairs={{0,96},{32,0},{64,32},{96,64},{1,97},{33,1},{65,33},{97,65},{2,98}... | collective-permute-start | bytes 786440 | tf_op jit(solution)/shard_map/ppermute | solution.py:12
  126.9 1.4 fusion.10
  128.3 10.7 %all-to-all-start.3 = ((bf16[32,8,2048]{2,1,0:T(8,128)(2,1)}), bf16[32,8,2048]{2,1,0:T(8,128)(2,1)S(1)}, u32[]{:S(2)}, u32[]{:S(2)}) async-start(bf16[32,8,2048]{2,1,0:T(8,128)(2,1)} %fusion.10), calls=%async_computation.3 | async-start | bytes 2097152 | tf_op jit(solution)/shard_map/all_to_all | solution.py:42
  139.0 1.4 add_convert_fusion.3
  140.5 1.6 collective-permute-start.15
  142.2 11.7 %collective-permute-done.15 = bf16[128,2048]{1,0:T(8,128)(2,1)S(1)} collective-permute-done((bf16[128,2048]{1,0:T(8,128)(2,1)S(1)}, bf16[128,2048]{1,0:T(8,128)(2,1)S(1)}, u32[]{:S(2)}, u32[]{:S(2)}) %collective-permute-start.15) | collective-permute-done | bytes 524320 | tf_op jit(solution)/shard_map/ppermute | solution.py:12
  153.8 2.5 %collective-permute-done.13 = bf16[128,2048]{1,0:T(8,128)(2,1)S(1)} collective-permute-done((bf16[128,2048]{1,0:T(8,128)(2,1)S(1)}, bf16[128,2048]{1,0:T(8,128)(2,1)S(1)}, u32[]{:S(2)}, u32[]{:S(2)}) %collective-permute-start.13) | collective-permute-done | bytes 524320 | tf_op jit(solution)/shard_map/ppermute | solution.py:12
  156.3 2.6 %fusion.11 = bf16[32,8,2048]{2,1,0:T(8,128)(2,1)} fusion(bf16[128,2048]{1,0:T(8,128)(2,1)S(1)} %collective-permute-done.15, bf16[128,2048]{1,0:T(8,128)(2,1)S(1)} %collective-permute-done.13, f32[512,2048]{1,0:T(8,128)} %copy-done.1, s32[128]{0:T(128)S(1)} %multiply_add_fusion), kind=kOutput, calls=%fused_computation.21 | convolution fusion | flops 136085504 | bytes 3146240 | tf_op jit(solution)/shard_map/dot_general | solution.py:76
  159.0 8.4 %all-to-all-start.4 = ((bf16[32,8,2048]{2,1,0:T(8,128)(2,1)}), bf16[32,8,2048]{2,1,0:T(8,128)(2,1)S(1)}, u32[]{:S(2)}, u32[]{:S(2)}) async-start(bf16[32,8,2048]{2,1,0:T(8,128)(2,1)} %fusion.11), calls=%async_computation.4 | async-start | bytes 2097152 | tf_op jit(solution)/shard_map/all_to_all | solution.py:42
  167.4 6.4 %convert_bitcast_fusion.1 = bf16[1,2048,1024]{2,1,0:T(8,128)(2,1)} fusion(bf16[512,2048]{1,0:T(8,128)(2,1)} %copy-done.4, bf16[512,1024]{1,0:T(8,128)(2,1)} %copy-done.12), kind=kOutput, calls=%fused_computation.9 | convolution fusion | flops 2149580800 | bytes 7340032 | tf_op jit(solution)/shard_map/dot_general | solution.py:111
  173.8 4.6 %convert_bitcast_fusion = bf16[1,1024,2048]{2,1,0:T(8,128)(2,1)} fusion(bf16[512,2048]{1,0:T(8,128)(2,1)S(1)} %copy-done.6, f32[512,1024]{1,0:T(8,128)S(1)} %copy-done.11), kind=kOutput, calls=%fused_computation.8 | convolution fusion | flops 2154299392 | bytes 8388608 | tf_op jit(solution)/shard_map/dot_general | solution.py:114
  178.4 1.5 convolution_convert_fusion.3
  179.9 4.6 %all-to-all-done.4 = bf16[32,8,2048]{2,1,0:T(8,128)(2,1)S(1)} async-done(((bf16[32,8,2048]{2,1,0:T(8,128)(2,1)}), bf16[32,8,2048]{2,1,0:T(8,128)(2,1)S(1)}, u32[]{:S(2)}, u32[]{:S(2)}) %all-to-all-start.4) | async-done | bytes 1048608 | tf_op jit(solution)/shard_map/all_to_all | solution.py:42
  184.6 1.5 convolution_convert_fusion.2
  (65 shorter events, 2.5 us)
Async XLA Ops:
  0.6 19.3 %copy-start = (bf16[256,2048]{1,0:T(8,128)(2,1)S(1)}, bf16[256,2048]{1,0:T(8,128)(2,1)}, u32[]{:S(2)}) copy-start(bf16[256,2048]{1,0:T(8,128)(2,1)} %param.6) | copy-start | bytes 3145732
  2.6 17.2 %all-to-all-start = ((f32[32,8,128]{2,1,0:T(8,128)}), f32[32,8,128]{2,1,0:T(8,128)S(1)}, u32[]{:S(2)}, u32[]{:S(2)}) async-start(f32[32,8,128]{2,1,0:T(8,128)} %broadcast_in_dim.20), calls=%async_computation | async-start | bytes 262144 | tf_op jit(solution)/shard_map/all_to_all | solution.py:42
  19.9 21.3 %copy-start.3 = (bf16[256,2048]{1,0:T(8,128)(2,1)S(1)}, bf16[256,2048]{1,0:T(8,128)(2,1)}, u32[]{:S(2)}) copy-start(bf16[256,2048]{1,0:T(8,128)(2,1)} %param.7) | copy-start | bytes 3145732
  42.7 23.1 %copy-start.7 = (f32[1,1,128]{2,1,0:T(1,128)S(1)}, f32[1,1,128]{2,1,0:T(1,128)}, u32[]{:S(2)}) copy-start(f32[1,1,128]{2,1,0:T(1,128)} %param.9) | copy-start | bytes 1540
  42.7 23.1 %all-to-all-start.2 = ((bf16[32,8,2048]{2,1,0:T(8,128)(2,1)}), bf16[32,8,2048]{2,1,0:T(8,128)(2,1)S(1)}, u32[]{:S(2)}, u32[]{:S(2)}) async-start(bf16[32,8,2048]{2,1,0:T(8,128)(2,1)} %fusion.9), calls=%async_computation.2 | async-start | bytes 2097152 | tf_op jit(solution)/shard_map/all_to_all | solution.py:42
  47.2 15.9 %copy-start.2 = (bf16[128,2048]{1,0:T(8,128)(2,1)}, bf16[128,2048]{1,0:T(8,128)(2,1)S(1)}, u32[]{:S(2)}) copy-start(bf16[128,2048]{1,0:T(8,128)(2,1)S(1)} %convolution_convert_fusion.6) | copy-start | bytes 1572868
  47.2 14.4 %collective-permute-start = (bf16[128,2048]{1,0:T(8,128)(2,1)S(1)}, bf16[128,2048]{1,0:T(8,128)(2,1)S(1)}, u32[]{:S(2)}, u32[]{:S(2)}) collective-permute-start(bf16[128,2048]{1,0:T(8,128)(2,1)S(1)} %convolution_convert_fusion.6), channel_id=1, source_target_pairs={{0,32},{32,64},{64,96},{96,0},{1,33},{33,65},{65,97},{97,1},{2,34}... | collective-permute-start | bytes 1572872 | tf_op jit(solution)/shard_map/ppermute | solution.py:12
  48.5 13.9 %collective-permute-start.1 = (bf16[128,2048]{1,0:T(8,128)(2,1)S(1)}, bf16[128,2048]{1,0:T(8,128)(2,1)S(1)}, u32[]{:S(2)}, u32[]{:S(2)}) collective-permute-start(bf16[128,2048]{1,0:T(8,128)(2,1)S(1)} %convolution_convert_fusion.6), channel_id=1, source_target_pairs={{0,96},{32,0},{64,32},{96,64},{1,97},{33,1},{65,33},{97,65},{2,98}... | collective-permute-start | bytes 1572872 | tf_op jit(solution)/shard_map/ppermute | solution.py:12
  62.3 8.0 %collective-permute-start.2 = (bf16[64,2048]{1,0:T(8,128)(2,1)}, bf16[64,2048]{1,0:T(8,128)(2,1)S(1)}, u32[]{:S(2)}, u32[]{:S(2)}) collective-permute-start(bf16[64,2048]{1,0:T(8,128)(2,1)} %slice.85), channel_id=1, source_target_pairs={{0,32},{32,64},{64,96},{96,0},{1,33},{33,65},{65,97},{97,1},{2,34}... | collective-permute-start | bytes 786440 | tf_op jit(solution)/shard_map/ppermute | solution.py:12
  63.1 7.3 %collective-permute-start.3 = (bf16[64,2048]{1,0:T(8,128)(2,1)}, bf16[64,2048]{1,0:T(8,128)(2,1)}, u32[]{:S(2)}, u32[]{:S(2)}) collective-permute-start(bf16[64,2048]{1,0:T(8,128)(2,1)} %slice.86), channel_id=1, source_target_pairs={{0,96},{32,0},{64,32},{96,64},{1,97},{33,1},{65,33},{97,65},{2,98}... | collective-permute-start | bytes 786440 | tf_op jit(solution)/shard_map/ppermute | solution.py:12
  71.5 2.6 %copy-start.9 = (bf16[1,2048,1024]{2,1,0:T(8,128)(2,1)S(1)}, bf16[1,2048,1024]{2,1,0:T(8,128)(2,1)}, u32[]{:S(2)}) copy-start(bf16[1,2048,1024]{2,1,0:T(8,128)(2,1)} %param.10) | copy-start | bytes 12582916
  72.8 1.3 copy-start.4
  74.1 2.4 %copy-start.8 = (bf16[1,1024,2048]{2,1,0:T(8,128)(2,1)S(1)}, bf16[1,1024,2048]{2,1,0:T(8,128)(2,1)}, u32[]{:S(2)}) copy-start(bf16[1,1024,2048]{2,1,0:T(8,128)(2,1)} %param.11) | copy-start | bytes 12582916
  76.5 38.3 %copy-start.10 = (f32[512,1024]{1,0:T(8,128)}, f32[512,1024]{1,0:T(8,128)S(1)}, u32[]{:S(2)}) copy-start(f32[512,1024]{1,0:T(8,128)S(1)} %fusion.6) | copy-start | bytes 6291460
  79.1 7.5 %collective-permute-start.4 = (bf16[64,2048]{1,0:T(8,128)(2,1)S(1)}, bf16[64,2048]{1,0:T(8,128)(2,1)S(1)}, u32[]{:S(2)}, u32[]{:S(2)}) collective-permute-start(bf16[64,2048]{1,0:T(8,128)(2,1)S(1)} %get-tuple-element.32), channel_id=1, source_target_pairs={{0,32},{32,64},{64,96},{96,0},{1,33},{33,65},{65,97},{97,1},{2,34}... | collective-permute-start | bytes 786440 | tf_op jit(solution)/shard_map/ppermute | solution.py:12
  79.8 6.9 %collective-permute-start.6 = (bf16[64,2048]{1,0:T(8,128)(2,1)S(1)}, bf16[64,2048]{1,0:T(8,128)(2,1)S(1)}, u32[]{:S(2)}, u32[]{:S(2)}) collective-permute-start(bf16[64,2048]{1,0:T(8,128)(2,1)S(1)} %get-tuple-element.33), channel_id=1, source_target_pairs={{0,96},{32,0},{64,32},{96,64},{1,97},{33,1},{65,33},{97,65},{2,98}... | collective-permute-start | bytes 786440 | tf_op jit(solution)/shard_map/ppermute | solution.py:12
  82.5 15.4 %collective-permute-start.8 = (bf16[128,2048]{1,0:T(8,128)(2,1)S(1)}, bf16[128,2048]{1,0:T(8,128)(2,1)S(1)}, u32[]{:S(2)}, u32[]{:S(2)}) collective-permute-start(bf16[128,2048]{1,0:T(8,128)(2,1)S(1)} %fusion.12), channel_id=1, source_target_pairs={{0,32},{32,64},{64,96},{96,0},{1,33},{33,65},{65,97},{97,1},{2,34}... | collective-permute-start | bytes 1572872 | tf_op jit(solution)/shard_map/ppermute | solution.py:12
  82.5 15.5 %collective-permute-start.9 = (bf16[128,2048]{1,0:T(8,128)(2,1)S(1)}, bf16[128,2048]{1,0:T(8,128)(2,1)S(1)}, u32[]{:S(2)}, u32[]{:S(2)}) collective-permute-start(bf16[128,2048]{1,0:T(8,128)(2,1)S(1)} %fusion.12), channel_id=1, source_target_pairs={{0,96},{32,0},{64,32},{96,64},{1,97},{33,1},{65,33},{97,65},{2,98}... | collective-permute-start | bytes 1572872 | tf_op jit(solution)/shard_map/ppermute | solution.py:12
  86.9 35.2 %collective-permute-start.7 = (bf16[128,2048]{1,0:T(8,128)(2,1)S(1)}, bf16[128,2048]{1,0:T(8,128)(2,1)S(1)}, u32[]{:S(2)}, u32[]{:S(2)}) collective-permute-start(bf16[128,2048]{1,0:T(8,128)(2,1)S(1)} %pad_maximum_fusion.1), channel_id=1, source_target_pairs={{0,96},{32,0},{64,32},{96,64},{1,97},{33,1},{65,33},{97,65},{2,98}... | collective-permute-start | bytes 1572872 | tf_op jit(solution)/shard_map/ppermute | solution.py:12
  89.3 32.8 %collective-permute-start.5 = (bf16[128,2048]{1,0:T(8,128)(2,1)S(1)}, bf16[128,2048]{1,0:T(8,128)(2,1)S(1)}, u32[]{:S(2)}, u32[]{:S(2)}) collective-permute-start(bf16[128,2048]{1,0:T(8,128)(2,1)S(1)} %pad_maximum_fusion), channel_id=1, source_target_pairs={{0,32},{32,64},{64,96},{96,0},{1,33},{33,65},{65,97},{97,1},{2,34}... | collective-permute-start | bytes 1572872 | tf_op jit(solution)/shard_map/ppermute | solution.py:12
  97.9 16.8 %collective-permute-start.10 = (bf16[64,2048]{1,0:T(8,128)(2,1)S(1)}, bf16[64,2048]{1,0:T(8,128)(2,1)S(1)}, u32[]{:S(2)}, u32[]{:S(2)}) collective-permute-start(bf16[64,2048]{1,0:T(8,128)(2,1)S(1)} %slice.93), channel_id=1, source_target_pairs={{0,32},{32,64},{64,96},{96,0},{1,33},{33,65},{65,97},{97,1},{2,34}... | collective-permute-start | bytes 786440 | tf_op jit(solution)/shard_map/ppermute | solution.py:12
  98.1 16.7 %collective-permute-start.11 = (bf16[64,2048]{1,0:T(8,128)(2,1)S(1)}, bf16[64,2048]{1,0:T(8,128)(2,1)S(1)}, u32[]{:S(2)}, u32[]{:S(2)}) collective-permute-start(bf16[64,2048]{1,0:T(8,128)(2,1)S(1)} %slice.94), channel_id=1, source_target_pairs={{0,96},{32,0},{64,32},{96,64},{1,97},{33,1},{65,33},{97,65},{2,98}... | collective-permute-start | bytes 786440 | tf_op jit(solution)/shard_map/ppermute | solution.py:12
  114.8 1.4 copy-start.5
  119.7 2.4 %copy-start.12 = (bf16[512,1024]{1,0:T(8,128)(2,1)}, bf16[512,1024]{1,0:T(8,128)(2,1)S(1)}, u32[]{:S(2)}) copy-start(bf16[512,1024]{1,0:T(8,128)(2,1)S(1)} %fusion.19) | copy-start | bytes 3145732
  122.1 2.0 %copy-start.1 = (f32[512,2048]{1,0:T(8,128)}, f32[512,2048]{1,0:T(8,128)S(1)}, u32[]{:S(2)}) copy-start(f32[512,2048]{1,0:T(8,128)S(1)} %fusion.4) | copy-start | bytes 12582916
  124.2 14.8 %collective-permute-start.12 = (bf16[64,2048]{1,0:T(8,128)(2,1)S(1)}, bf16[64,2048]{1,0:T(8,128)(2,1)S(1)}, u32[]{:S(2)}, u32[]{:S(2)}) collective-permute-start(bf16[64,2048]{1,0:T(8,128)(2,1)S(1)} %get-tuple-element.28), channel_id=1, source_target_pairs={{0,32},{32,64},{64,96},{96,0},{1,33},{33,65},{65,97},{97,1},{2,34}... | collective-permute-start | bytes 786440 | tf_op jit(solution)/shard_map/ppermute | solution.py:12
  124.8 14.2 %collective-permute-start.14 = (bf16[64,2048]{1,0:T(8,128)(2,1)S(1)}, bf16[64,2048]{1,0:T(8,128)(2,1)}, u32[]{:S(2)}, u32[]{:S(2)}) collective-permute-start(bf16[64,2048]{1,0:T(8,128)(2,1)S(1)} %get-tuple-element.29), channel_id=1, source_target_pairs={{0,96},{32,0},{64,32},{96,64},{1,97},{33,1},{65,33},{97,65},{2,98}... | collective-permute-start | bytes 786440 | tf_op jit(solution)/shard_map/ppermute | solution.py:12
  128.3 30.7 %all-to-all-start.3 = ((bf16[32,8,2048]{2,1,0:T(8,128)(2,1)}), bf16[32,8,2048]{2,1,0:T(8,128)(2,1)S(1)}, u32[]{:S(2)}, u32[]{:S(2)}) async-start(bf16[32,8,2048]{2,1,0:T(8,128)(2,1)} %fusion.10), calls=%async_computation.3 | async-start | bytes 2097152 | tf_op jit(solution)/shard_map/all_to_all | solution.py:42
  140.5 13.4 %collective-permute-start.15 = (bf16[128,2048]{1,0:T(8,128)(2,1)S(1)}, bf16[128,2048]{1,0:T(8,128)(2,1)S(1)}, u32[]{:S(2)}, u32[]{:S(2)}) collective-permute-start(bf16[128,2048]{1,0:T(8,128)(2,1)S(1)} %pad_maximum_fusion.3), channel_id=1, source_target_pairs={{0,96},{32,0},{64,32},{96,64},{1,97},{33,1},{65,33},{97,65},{2,98}... | collective-permute-start | bytes 1572872 | tf_op jit(solution)/shard_map/ppermute | solution.py:12
  142.1 14.3 %collective-permute-start.13 = (bf16[128,2048]{1,0:T(8,128)(2,1)S(1)}, bf16[128,2048]{1,0:T(8,128)(2,1)S(1)}, u32[]{:S(2)}, u32[]{:S(2)}) collective-permute-start(bf16[128,2048]{1,0:T(8,128)(2,1)S(1)} %pad_maximum_fusion.2), channel_id=1, source_target_pairs={{0,32},{32,64},{64,96},{96,0},{1,33},{33,65},{65,97},{97,1},{2,34}... | collective-permute-start | bytes 1572872 | tf_op jit(solution)/shard_map/ppermute | solution.py:12
  159.0 25.6 %all-to-all-start.4 = ((bf16[32,8,2048]{2,1,0:T(8,128)(2,1)}), bf16[32,8,2048]{2,1,0:T(8,128)(2,1)S(1)}, u32[]{:S(2)}, u32[]{:S(2)}) async-start(bf16[32,8,2048]{2,1,0:T(8,128)(2,1)} %fusion.11), calls=%async_computation.4 | async-start | bytes 2097152 | tf_op jit(solution)/shard_map/all_to_all | solution.py:42
  167.4 6.4 %copy-start.6 = (bf16[512,2048]{1,0:T(8,128)(2,1)S(1)}, bf16[512,2048]{1,0:T(8,128)(2,1)}, u32[]{:S(2)}) copy-start(bf16[512,2048]{1,0:T(8,128)(2,1)} %copy-done.5) | copy-start | bytes 6291460
  167.4 6.4 %copy-start.11 = (f32[512,1024]{1,0:T(8,128)S(1)}, f32[512,1024]{1,0:T(8,128)}, u32[]{:S(2)}) copy-start(f32[512,1024]{1,0:T(8,128)} %copy-done.10) | copy-start | bytes 6291460

commit v2 on v1

--- a/solution.py
+++ b/solution.py
@@ -1,6 +1,10 @@
+import functools
+
 import jax
 import jax.numpy as jnp
 from jax import lax
+from jax.experimental import pallas as pl
+from jax.experimental.pallas import tpu as pltpu
 from jax.sharding import PartitionSpec as P
 
 F32 = jnp.float32
@@ -42,6 +46,22 @@
     return lax.all_to_all(array, "expert", split_axis=0, concat_axis=0, tiled=True)
 
 
+def ask_kernel(tok_dev, slot_size, picks, wanted):
+    capacity, slots = picks.shape[1], wanted.shape[0]
+    own = picks[...]
+    source = own // tok_dev
+    square = (capacity, capacity)
+    down = lax.broadcasted_iota(jnp.int32, square, 0)
+    across = lax.broadcasted_iota(jnp.int32, square, 1)
+    turned = jnp.sum(jnp.where(down == across, source, 0), axis=1, keepdims=True)
+    earlier = (turned == source) & (down < across)
+    rank = jnp.sum(earlier.astype(jnp.int32), axis=0, keepdims=True)
+    slot = lax.broadcasted_iota(jnp.int32, (slots, capacity), 0)
+    here = slot == source * slot_size + rank
+    token = jnp.sum(jnp.where(here, own - source * tok_dev + 1, 0), axis=1, keepdims=True)
+    wanted[...] = jnp.broadcast_to(token.astype(F32), wanted.shape)
+
+
 def on_device(tokens, out_grad, picks, gates, w_in, w_out):
     experts = lax.axis_size("expert")
     tok_dev, width = tokens.shape
@@ -56,8 +76,11 @@
     rank = jnp.sum(earlier.astype(jnp.int32), axis=1)
     slot_of = source * slot_size + rank
     place = slot_of[None, :] == jnp.arange(slots, dtype=jnp.int32)[:, None]
-    wanted = jnp.sum(jnp.where(place, own_picks[None, :] % tok_dev + 1, 0), axis=1)
-    wanted = jnp.broadcast_to(wanted.astype(F32)[:, None], (slots, 128))
+    wanted = pl.pallas_call(
+        functools.partial(ask_kernel, tok_dev, slot_size),
+        out_shape=jax.ShapeDtypeStruct((slots, 128), F32),
+        compiler_params=pltpu.CompilerParams(vmem_limit_bytes=4 * 2**20),
+    )(picks[0])
     place = place.astype(BF16)
 
     asked = swap(wanted.reshape(experts, slot_size, 128)).reshape(slots, 128)[:, :1]
@@ -65,9 +88,9 @@
         asked.astype(jnp.int32) == jnp.arange(1, tok_dev + 1, dtype=jnp.int32)[None, :]
     ).astype(BF16)
 
-    def send(rows):
+    def pack(rows):
         packed = jnp.dot(layout, rows, preferred_element_type=F32).astype(BF16)
-        return swap(packed.reshape(experts, slot_size, width)).reshape(slots, width)
+        return packed.reshape(experts, slot_size, width)
 
     def unslot(rows):
         return lax.dot_general(place, rows, (((0,), (0,)), ((), ())), preferred_element_type=F32)
@@ -83,20 +106,22 @@
     weight_in = w_in[0]
     weight_out = w_out[0]
 
-    came_in = send(tokens)
-    came_in, out_grad = lax.optimization_barrier((came_in, out_grad))
-    came_cot = send(out_grad)
+    came_in = swap(pack(tokens)).reshape(slots, width)
+    packed_cot, came_in = lax.optimization_barrier((pack(out_grad), came_in))
+    came_cot = swap(packed_cot).reshape(slots, width)
     inputs = ring_gather(unslot(came_in).astype(BF16))
+    inputs = jnp.concatenate(inputs, axis=0)
+    came_cot, inputs = lax.optimization_barrier((came_cot, inputs))
     dout_own = (own_gates * unslot(came_cot)).astype(BF16)
     dout_own, inputs = lax.optimization_barrier((dout_own, inputs))
     dout = ring_gather(dout_own)
-    inputs = jnp.concatenate(inputs, axis=0)
-    dout = jnp.concatenate(dout, axis=0)
 
     act = jnp.dot(inputs, weight_in, preferred_element_type=F32)
     hidden, gelu_back = jax.vjp(jax.nn.gelu, act)
     hidden = hidden.astype(BF16)
     part = jnp.dot(hidden, weight_out, preferred_element_type=F32)
+    part, *near = lax.optimization_barrier((part, *dout[:3]))
+    dout = jnp.concatenate([*near, *dout[3:]], axis=0)
     summed = ring_sum(part)
     outputs = (own_gates * summed).astype(BF16)
 

time: 187 us -> 167 us (0.89)
  blocking collectives: 20.8 us -> 0 us
  matrix products: 31.5 us -> 36.2 us
  waiting for transfers between devices: 66.2 us -> 62.5 us
  starting transfers between devices: 54.1 us -> 57.6 us
  local copies, waits for them, and re-layouts: 9.12 us -> 5.67 us
    all_to_all x1 -> x0, blocking collectives: 20.8 us -> none  [swap(): lax.all_to_all(array, 'expert', split_axis=0, concat_axis=0, tiled=True)]
    ppermute x16, waiting for transfers between devices: 53.9 us -> 34.1 us  [shifted(): lax.ppermute(array, 'dp', [(i, (i + step) % count) for i in range(count)])]
    all_to_all x4 -> x5, waiting for transfers between devices: 12.2 us -> 28.5 us  [swap(): lax.all_to_all(array, 'expert', split_axis=0, concat_axis=0, tiled=True)]
    dot_general x1, matrix products: 2.39 us -> 5.15 us  [on_device(): act = jnp.dot(inputs, weight_in, preferred_element_type=F32)]
    all_to_all x4 -> x5, starting transfers between devices: 32.8 us -> 35.5 us  [swap(): lax.all_to_all(array, 'expert', split_axis=0, concat_axis=0, tiled=True)]
  transfers between devices with their start and end apart: 20 -> 21, of which waited for: 9 -> 12; matrix products, arithmetic and copies ran while one was open for 14% -> 22% of each run, Pallas kernels for 0% -> 0%
where the time goes in v2:
time: 167 us
  waiting for transfers between devices  62.5 us (37%)
  starting transfers between devices  57.6 us (34%)
  matrix products  36.2 us (22%)
  local copies, waits for them, and re-layouts  5.67 us (3%)
  other arithmetic  2.8 us (2%)
    all_to_all x5, starting transfers between devices, swap(): lax.all_to_all(array, 'expert', split_axis=0, concat_axis=0, tiled=True)  35.5 us
    ppermute x16, waiting for transfers between devices, shifted(): lax.ppermute(array, 'dp', [(i, (i + step) % count) for i in range(count)])  34.1 us
    all_to_all x5, waiting for transfers between devices, swap(): lax.all_to_all(array, 'expert', split_axis=0, concat_axis=0, tiled=True)  28.5 us
    ppermute x16, starting transfers between devices, shifted(): lax.ppermute(array, 'dp', [(i, (i + step) % count) for i in range(count)])  22.1 us
    dot_general x1, matrix products, on_device(): lax.dot_general(inputs, dact, (((0,), (0,)), ((), ())), preferred_element...  6.4 us
    dot_general x1, matrix products, on_device(): act = jnp.dot(inputs, weight_in, preferred_element_type=F32)  5.15 us
    unnamed x33, local copies, waits for them, and re-layouts  4.63 us
    dot_general x1, matrix products, on_device(): lax.dot_general(hidden, dout, (((0,), (0,)), ((), ())), preferred_element...  4.61 us
  transfers between devices with their start and end apart: 21, of which 12 were waited for; matrix products, arithmetic and copies ran while one was open for 22% of the time, Pallas kernels for 0%

profile of v2, /device:TPU:1, one launch (start us, length us, event | category | flops | bytes accessed | tf_op | source)
XLA Modules:
  0.0 166.8 jit_solution(1118770175587505154)
XLA Ops:
  0.7 0.7 copy-done.1
  1.4 0.9 shard_map.93
  2.3 9.6 %all-to-all-start = ((f32[32,8,128]{2,1,0:T(8,128)}), f32[32,8,128]{2,1,0:T(8,128)S(1)}, u32[]{:S(2)}, u32[]{:S(2)}) async-start(f32[32,8,128]{2,1,0:T(8,128)} %bitcast.1), calls=%async_computation | async-start | bytes 262144 | tf_op jit(solution)/shard_map/all_to_all | solution.py:46
  11.9 7.6 %all-to-all-done = f32[32,8,128]{2,1,0:T(8,128)S(1)} async-done(((f32[32,8,128]{2,1,0:T(8,128)}), f32[32,8,128]{2,1,0:T(8,128)S(1)}, u32[]{:S(2)}, u32[]{:S(2)}) %all-to-all-start) | async-done | bytes 131104 | tf_op jit(solution)/shard_map/all_to_all | solution.py:46
  19.7 1.4 fusion.9
  21.2 4.0 %all-to-all-start.1 = ((bf16[32,8,2048]{2,1,0:T(8,128)(2,1)}), bf16[32,8,2048]{2,1,0:T(8,128)(2,1)S(1)}, u32[]{:S(2)}, u32[]{:S(2)}) async-start(bf16[32,8,2048]{2,1,0:T(8,128)(2,1)} %fusion.9), calls=%async_computation.1 | async-start | bytes 2097152 | tf_op jit(solution)/shard_map/all_to_all | solution.py:46
  25.4 1.5 fusion.8
  26.9 15.6 %all-to-all-done.1 = bf16[32,8,2048]{2,1,0:T(8,128)(2,1)S(1)} async-done(((bf16[32,8,2048]{2,1,0:T(8,128)(2,1)}), bf16[32,8,2048]{2,1,0:T(8,128)(2,1)S(1)}, u32[]{:S(2)}, u32[]{:S(2)}) %all-to-all-start.1) | async-done | bytes 1048608 | tf_op jit(solution)/shard_map/all_to_all | solution.py:46
  42.5 1.3 constant_dynamic-update-slice_fusion.4
  43.8 1.2 collective-permute-start
  45.0 1.5 collective-permute-start.1
  46.5 4.5 %all-to-all-start.2 = ((bf16[32,8,2048]{2,1,0:T(8,128)(2,1)}), bf16[32,8,2048]{2,1,0:T(8,128)(2,1)S(1)}, u32[]{:S(2)}, u32[]{:S(2)}) async-start(bf16[32,8,2048]{2,1,0:T(8,128)(2,1)} %fusion.8), calls=%async_computation.2 | async-start | bytes 2097152 | tf_op jit(solution)/shard_map/all_to_all | solution.py:46
  51.0 7.3 %collective-permute-done = bf16[128,2048]{1,0:T(8,128)(2,1)S(1)} collective-permute-done((bf16[128,2048]{1,0:T(8,128)(2,1)}, bf16[128,2048]{1,0:T(8,128)(2,1)S(1)}, u32[]{:S(2)}, u32[]{:S(2)}) %collective-permute-start) | collective-permute-done | bytes 524320 | tf_op jit(solution)/shard_map/ppermute | solution.py:16
  58.5 2.7 %collective-permute-start.3 = (bf16[64,2048]{1,0:T(8,128)(2,1)S(1)}, bf16[64,2048]{1,0:T(8,128)(2,1)S(1)}, u32[]{:S(2)}, u32[]{:S(2)}) collective-permute-start(bf16[64,2048]{1,0:T(8,128)(2,1)S(1)} %slice.86), channel_id=1, source_target_pairs={{0,96},{32,0},{64,32},{96,64},{1,97},{33,1},{65,33},{97,65},{2,98}... | collective-permute-start | bytes 786440 | tf_op jit(solution)/shard_map/ppermute | solution.py:16
  61.2 0.8 constant_dynamic-update-slice_fusion.3
  62.0 0.8 constant_dynamic-update-slice_fusion.2
  62.8 3.3 %collective-permute-done.2 = bf16[64,2048]{1,0:T(8,128)(2,1)S(1)} collective-permute-done((bf16[64,2048]{1,0:T(8,128)(2,1)S(1)}, bf16[64,2048]{1,0:T(8,128)(2,1)S(1)}, u32[]{:S(2)}, u32[]{:S(2)}) %collective-permute-start.2) | collective-permute-done | bytes 262176 | tf_op jit(solution)/shard_map/ppermute | solution.py:16
  66.2 0.7 constant_dynamic-update-slice_fusion.1
  66.9 0.7 constant_dynamic-update-slice_fusion
  67.6 0.6 all-to-all-done.2
  68.7 2.7 %collective-permute-start.5 = (bf16[128,2048]{1,0:T(8,128)(2,1)S(1)}, bf16[128,2048]{1,0:T(8,128)(2,1)S(1)}, u32[]{:S(2)}, u32[]{:S(2)}) collective-permute-start(bf16[128,2048]{1,0:T(8,128)(2,1)S(1)} %fusion.12), channel_id=1, source_target_pairs={{0,96},{32,0},{64,32},{96,64},{1,97},{33,1},{65,33},{97,65},{2,98}... | collective-permute-start | bytes 1572872 | tf_op jit(solution)/shard_map/ppermute | solution.py:16
  71.4 5.1 %fusion.6 = f32[512,1024]{1,0:T(8,128)S(1)} fusion(bf16[512,2048]{1,0:T(8,128)(2,1)} %constant_dynamic-update-slice_fusion, bf16[1,2048,1024]{2,1,0:T(8,128)(2,1)} %param.10), kind=kOutput, calls=%fused_computation.6 | convolution fusion | flops 2147483648 | bytes 8388608 | tf_op jit(solution)/shard_map/dot_general | solution.py:119
  76.6 2.5 %fusion.2 = f32[512,2048]{1,0:T(8,128)S(1)} fusion(bf16[1,1024,2048]{2,1,0:T(8,128)(2,1)S(1)} %copy-done.8, f32[512,1024]{1,0:T(8,128)S(1)} %fusion.6), kind=kOutput, calls=%fused_computation.2 | convolution fusion | flops 2152202240 | bytes 10485760 | tf_op jit(solution)/shard_map/dot_general | solution.py:122
  79.1 2.7 %collective-permute-done.4 = bf16[128,2048]{1,0:T(8,128)(2,1)S(1)} collective-permute-done((bf16[128,2048]{1,0:T(8,128)(2,1)S(1)}, bf16[128,2048]{1,0:T(8,128)(2,1)S(1)}, u32[]{:S(2)}, u32[]{:S(2)}) %collective-permute-start.4) | collective-permute-done | bytes 524320 | tf_op jit(solution)/shard_map/ppermute | solution.py:16
  82.4 2.7 %collective-permute-start.8 = (bf16[64,2048]{1,0:T(8,128)(2,1)S(1)}, bf16[64,2048]{1,0:T(8,128)(2,1)S(1)}, u32[]{:S(2)}, u32[]{:S(2)}) collective-permute-start(bf16[64,2048]{1,0:T(8,128)(2,1)S(1)} %get-tuple-element.37), channel_id=1, source_target_pairs={{0,96},{32,0},{64,32},{96,64},{1,97},{33,1},{65,33},{97,65},{2,98}... | collective-permute-start | bytes 786440 | tf_op jit(solution)/shard_map/ppermute | solution.py:16
  85.2 2.7 %collective-permute-start.11 = (bf16[64,2048]{1,0:T(8,128)(2,1)S(1)}, bf16[64,2048]{1,0:T(8,128)(2,1)S(1)}, u32[]{:S(2)}, u32[]{:S(2)}) collective-permute-start(bf16[64,2048]{1,0:T(8,128)(2,1)S(1)} %slice.92), channel_id=1, source_target_pairs={{0,96},{32,0},{64,32},{96,64},{1,97},{33,1},{65,33},{97,65},{2,98}... | collective-permute-start | bytes 786440 | tf_op jit(solution)/shard_map/ppermute | solution.py:16
  88.0 0.8 collective-permute-done.6
  89.0 2.7 %collective-permute-start.9 = (bf16[128,2048]{1,0:T(8,128)(2,1)S(1)}, bf16[128,2048]{1,0:T(8,128)(2,1)S(1)}, u32[]{:S(2)}, u32[]{:S(2)}) collective-permute-start(bf16[128,2048]{1,0:T(8,128)(2,1)S(1)} %pad_maximum_fusion.1), channel_id=1, source_target_pairs={{0,96},{32,0},{64,32},{96,64},{1,97},{33,1},{65,33},{97,65},{2,98}... | collective-permute-start | bytes 1572872 | tf_op jit(solution)/shard_map/ppermute | solution.py:16
  92.0 2.6 %collective-permute-done.10 = bf16[64,2048]{1,0:T(8,128)(2,1)S(1)} collective-permute-done((bf16[64,2048]{1,0:T(8,128)(2,1)S(1)}, bf16[64,2048]{1,0:T(8,128)(2,1)S(1)}, u32[]{:S(2)}, u32[]{:S(2)}) %collective-permute-start.10) | collective-permute-done | bytes 262176 | tf_op jit(solution)/shard_map/ppermute | solution.py:16
  94.7 1.3 copy-done.5
  96.0 3.4 %fusion.19 = bf16[512,1024]{1,0:T(8,128)(2,1)S(1)} fusion(f32[512,1024]{1,0:T(8,128)S(1)} %fusion.6, bf16[512,2048]{1,0:T(8,128)(2,1)S(1)} %constant_dynamic-update-slice_fusion.5, bf16[1,1024,2048]{2,1,0:T(8,128)(2,1)S(1)} %copy-done.8), kind=kOutput, calls=%fused_computation.31 | convolution fusion | flops 2157969408 | bytes 9437184 | tf_op jit(solution)/shard_map/dot_general | solution.py:128
  99.5 2.4 %fusion.4 = f32[512,2048]{1,0:T(8,128)S(1)} fusion(bf16[512,1024]{1,0:T(8,128)(2,1)S(1)} %fusion.19, bf16[1,2048,1024]{2,1,0:T(8,128)(2,1)S(1)} %copy-done.9), kind=kOutput, calls=%fused_computation.4 | convolution fusion | flops 2147483648 | bytes 9437184 | tf_op jit(solution)/shard_map/dot_general | solution.py:130
  101.9 3.1 %collective-permute-done.9 = bf16[128,2048]{1,0:T(8,128)(2,1)S(1)} collective-permute-done((bf16[128,2048]{1,0:T(8,128)(2,1)S(1)}, bf16[128,2048]{1,0:T(8,128)(2,1)S(1)}, u32[]{:S(2)}, u32[]{:S(2)}) %collective-permute-start.9) | collective-permute-done | bytes 524320 | tf_op jit(solution)/shard_map/ppermute | solution.py:16
  105.7 1.1 collective-permute-start.12
  106.8 2.4 %collective-permute-start.14 = (bf16[64,2048]{1,0:T(8,128)(2,1)S(1)}, bf16[64,2048]{1,0:T(8,128)(2,1)}, u32[]{:S(2)}, u32[]{:S(2)}) collective-permute-start(bf16[64,2048]{1,0:T(8,128)(2,1)S(1)} %get-tuple-element.33), channel_id=1, source_target_pairs={{0,96},{32,0},{64,32},{96,64},{1,97},{33,1},{65,33},{97,65},{2,98}... | collective-permute-start | bytes 786440 | tf_op jit(solution)/shard_map/ppermute | solution.py:16
  109.3 1.4 fusion.10
  110.6 8.9 %all-to-all-start.3 = ((bf16[32,8,2048]{2,1,0:T(8,128)(2,1)}), bf16[32,8,2048]{2,1,0:T(8,128)(2,1)S(1)}, u32[]{:S(2)}, u32[]{:S(2)}) async-start(bf16[32,8,2048]{2,1,0:T(8,128)(2,1)} %fusion.10), calls=%async_computation.3 | async-start | bytes 2097152 | tf_op jit(solution)/shard_map/all_to_all | solution.py:46
  119.6 1.4 add_convert_fusion.3
  121.1 1.7 %collective-permute-start.15 = (bf16[128,2048]{1,0:T(8,128)(2,1)S(1)}, bf16[128,2048]{1,0:T(8,128)(2,1)S(1)}, u32[]{:S(2)}, u32[]{:S(2)}) collective-permute-start(bf16[128,2048]{1,0:T(8,128)(2,1)S(1)} %pad_maximum_fusion.3), channel_id=1, source_target_pairs={{0,96},{32,0},{64,32},{96,64},{1,97},{33,1},{65,33},{97,65},{2,98}... | collective-permute-start | bytes 1572872 | tf_op jit(solution)/shard_map/ppermute | solution.py:16
  122.9 11.5 %collective-permute-done.15 = bf16[128,2048]{1,0:T(8,128)(2,1)S(1)} collective-permute-done((bf16[128,2048]{1,0:T(8,128)(2,1)S(1)}, bf16[128,2048]{1,0:T(8,128)(2,1)S(1)}, u32[]{:S(2)}, u32[]{:S(2)}) %collective-permute-start.15) | collective-permute-done | bytes 524320 | tf_op jit(solution)/shard_map/ppermute | solution.py:16
  134.4 2.6 %collective-permute-done.13 = bf16[128,2048]{1,0:T(8,128)(2,1)S(1)} collective-permute-done((bf16[128,2048]{1,0:T(8,128)(2,1)S(1)}, bf16[128,2048]{1,0:T(8,128)(2,1)S(1)}, u32[]{:S(2)}, u32[]{:S(2)}) %collective-permute-start.13) | collective-permute-done | bytes 524320 | tf_op jit(solution)/shard_map/ppermute | solution.py:16
  137.1 2.7 %fusion.11 = bf16[32,8,2048]{2,1,0:T(8,128)(2,1)} fusion(bf16[128,2048]{1,0:T(8,128)(2,1)S(1)} %collective-permute-done.15, bf16[128,2048]{1,0:T(8,128)(2,1)S(1)} %collective-permute-done.13, f32[512,2048]{1,0:T(8,128)} %copy-done.3, s32[128]{0:T(128)S(1)} %multiply_add_fusion), kind=kOutput, calls=%fused_computation.21 | convolution fusion | flops 136085504 | bytes 3146240 | tf_op jit(solution)/shard_map/dot_general | solution.py:99
  139.7 8.4 %all-to-all-start.4 = ((bf16[32,8,2048]{2,1,0:T(8,128)(2,1)}), bf16[32,8,2048]{2,1,0:T(8,128)(2,1)S(1)}, u32[]{:S(2)}, u32[]{:S(2)}) async-start(bf16[32,8,2048]{2,1,0:T(8,128)(2,1)} %fusion.11), calls=%async_computation.4 | async-start | bytes 2097152 | tf_op jit(solution)/shard_map/all_to_all | solution.py:46
  148.1 6.4 %convert_bitcast_fusion.1 = bf16[1,2048,1024]{2,1,0:T(8,128)(2,1)} fusion(bf16[512,2048]{1,0:T(8,128)(2,1)} %constant_dynamic-update-slice_fusion, bf16[512,1024]{1,0:T(8,128)(2,1)} %copy-done.12), kind=kOutput, calls=%fused_computation.9 | convolution fusion | flops 2149580800 | bytes 7340032 | tf_op jit(solution)/shard_map/dot_general | solution.py:136
  154.5 4.6 %convert_bitcast_fusion = bf16[1,1024,2048]{2,1,0:T(8,128)(2,1)} fusion(bf16[512,2048]{1,0:T(8,128)(2,1)S(1)} %copy-done.6, f32[512,1024]{1,0:T(8,128)S(1)} %copy-done.11), kind=kOutput, calls=%fused_computation.8 | convolution fusion | flops 2154299392 | bytes 8388608 | tf_op jit(solution)/shard_map/dot_general | solution.py:139
  159.2 1.5 convolution_convert_fusion.3
  160.7 4.6 %all-to-all-done.4 = bf16[32,8,2048]{2,1,0:T(8,128)(2,1)S(1)} async-done(((bf16[32,8,2048]{2,1,0:T(8,128)(2,1)}), bf16[32,8,2048]{2,1,0:T(8,128)(2,1)S(1)}, u32[]{:S(2)}, u32[]{:S(2)}) %all-to-all-start.4) | async-done | bytes 1048608 | tf_op jit(solution)/shard_map/all_to_all | solution.py:46
  165.3 1.5 convolution_convert_fusion.2
  (64 shorter events, 2.9 us)
Async XLA Ops:
  0.6 19.1 %copy-start = (bf16[256,2048]{1,0:T(8,128)(2,1)S(1)}, bf16[256,2048]{1,0:T(8,128)(2,1)}, u32[]{:S(2)}) copy-start(bf16[256,2048]{1,0:T(8,128)(2,1)} %param.6) | copy-start | bytes 3145732
  0.6 0.7 copy-start.1
  2.3 17.2 %all-to-all-start = ((f32[32,8,128]{2,1,0:T(8,128)}), f32[32,8,128]{2,1,0:T(8,128)S(1)}, u32[]{:S(2)}, u32[]{:S(2)}) async-start(f32[32,8,128]{2,1,0:T(8,128)} %bitcast.1), calls=%async_computation | async-start | bytes 262144 | tf_op jit(solution)/shard_map/all_to_all | solution.py:46
  19.7 5.5 %copy-start.2 = (s32[1,1,128]{2,1,0:T(1,128)S(1)}, s32[1,1,128]{2,1,0:T(1,128)}, u32[]{:S(2)}) copy-start(s32[1,1,128]{2,1,0:T(1,128)} %param.8) | copy-start | bytes 1540
  19.7 5.7 %copy-start.4 = (bf16[256,2048]{1,0:T(8,128)(2,1)S(1)}, bf16[256,2048]{1,0:T(8,128)(2,1)}, u32[]{:S(2)}) copy-start(bf16[256,2048]{1,0:T(8,128)(2,1)} %param.7) | copy-start | bytes 3145732
  21.2 21.3 %all-to-all-start.1 = ((bf16[32,8,2048]{2,1,0:T(8,128)(2,1)}), bf16[32,8,2048]{2,1,0:T(8,128)(2,1)S(1)}, u32[]{:S(2)}, u32[]{:S(2)}) async-start(bf16[32,8,2048]{2,1,0:T(8,128)(2,1)} %fusion.9), calls=%async_computation.1 | async-start | bytes 2097152 | tf_op jit(solution)/shard_map/all_to_all | solution.py:46
  43.8 14.5 %collective-permute-start = (bf16[128,2048]{1,0:T(8,128)(2,1)}, bf16[128,2048]{1,0:T(8,128)(2,1)S(1)}, u32[]{:S(2)}, u32[]{:S(2)}) collective-permute-start(bf16[128,2048]{1,0:T(8,128)(2,1)} %get-tuple-element.41), channel_id=1, source_target_pairs={{0,32},{32,64},{64,96},{96,0},{1,33},{33,65},{65,97},{97,1},{2,34}... | collective-permute-start | bytes 1572872 | tf_op jit(solution)/shard_map/ppermute | solution.py:16
  45.0 13.4 %collective-permute-start.1 = (bf16[128,2048]{1,0:T(8,128)(2,1)}, bf16[128,2048]{1,0:T(8,128)(2,1)S(1)}, u32[]{:S(2)}, u32[]{:S(2)}) collective-permute-start(bf16[128,2048]{1,0:T(8,128)(2,1)} %get-tuple-element.41), channel_id=1, source_target_pairs={{0,96},{32,0},{64,32},{96,64},{1,97},{33,1},{65,33},{97,65},{2,98}... | collective-permute-start | bytes 1572872 | tf_op jit(solution)/shard_map/ppermute | solution.py:16
  46.5 21.8 %all-to-all-start.2 = ((bf16[32,8,2048]{2,1,0:T(8,128)(2,1)}), bf16[32,8,2048]{2,1,0:T(8,128)(2,1)S(1)}, u32[]{:S(2)}, u32[]{:S(2)}) async-start(bf16[32,8,2048]{2,1,0:T(8,128)(2,1)} %fusion.8), calls=%async_computation.2 | async-start | bytes 2097152 | tf_op jit(solution)/shard_map/all_to_all | solution.py:46
  51.0 17.3 %copy-start.7 = (f32[1,1,128]{2,1,0:T(1,128)S(1)}, f32[1,1,128]{2,1,0:T(1,128)}, u32[]{:S(2)}) copy-start(f32[1,1,128]{2,1,0:T(1,128)} %param.9) | copy-start | bytes 1540
  58.3 7.9 %collective-permute-start.2 = (bf16[64,2048]{1,0:T(8,128)(2,1)S(1)}, bf16[64,2048]{1,0:T(8,128)(2,1)S(1)}, u32[]{:S(2)}, u32[]{:S(2)}) collective-permute-start(bf16[64,2048]{1,0:T(8,128)(2,1)S(1)} %slice.85), channel_id=1, source_target_pairs={{0,32},{32,64},{64,96},{96,0},{1,33},{33,65},{65,97},{97,1},{2,34}... | collective-permute-start | bytes 786440 | tf_op jit(solution)/shard_map/ppermute | solution.py:16
  58.5 8.4 %collective-permute-start.3 = (bf16[64,2048]{1,0:T(8,128)(2,1)S(1)}, bf16[64,2048]{1,0:T(8,128)(2,1)S(1)}, u32[]{:S(2)}, u32[]{:S(2)}) collective-permute-start(bf16[64,2048]{1,0:T(8,128)(2,1)S(1)} %slice.86), channel_id=1, source_target_pairs={{0,96},{32,0},{64,32},{96,64},{1,97},{33,1},{65,33},{97,65},{2,98}... | collective-permute-start | bytes 786440 | tf_op jit(solution)/shard_map/ppermute | solution.py:16
  68.7 7.9 %copy-start.8 = (bf16[1,1024,2048]{2,1,0:T(8,128)(2,1)S(1)}, bf16[1,1024,2048]{2,1,0:T(8,128)(2,1)}, u32[]{:S(2)}) copy-start(bf16[1,1024,2048]{2,1,0:T(8,128)(2,1)} %param.11) | copy-start | bytes 12582916
  68.7 13.2 %collective-permute-start.4 = (bf16[128,2048]{1,0:T(8,128)(2,1)S(1)}, bf16[128,2048]{1,0:T(8,128)(2,1)S(1)}, u32[]{:S(2)}, u32[]{:S(2)}) collective-permute-start(bf16[128,2048]{1,0:T(8,128)(2,1)S(1)} %fusion.12), channel_id=1, source_target_pairs={{0,32},{32,64},{64,96},{96,0},{1,33},{33,65},{65,97},{97,1},{2,34}... | collective-permute-start | bytes 1572872 | tf_op jit(solution)/shard_map/ppermute | solution.py:16
  68.7 13.1 %collective-permute-start.5 = (bf16[128,2048]{1,0:T(8,128)(2,1)S(1)}, bf16[128,2048]{1,0:T(8,128)(2,1)S(1)}, u32[]{:S(2)}, u32[]{:S(2)}) collective-permute-start(bf16[128,2048]{1,0:T(8,128)(2,1)S(1)} %fusion.12), channel_id=1, source_target_pairs={{0,96},{32,0},{64,32},{96,64},{1,97},{33,1},{65,33},{97,65},{2,98}... | collective-permute-start | bytes 1572872 | tf_op jit(solution)/shard_map/ppermute | solution.py:16
  76.6 18.1 %copy-start.10 = (f32[512,1024]{1,0:T(8,128)}, f32[512,1024]{1,0:T(8,128)S(1)}, u32[]{:S(2)}) copy-start(f32[512,1024]{1,0:T(8,128)S(1)} %fusion.6) | copy-start | bytes 6291460
  82.3 6.5 %collective-permute-start.6 = (bf16[64,2048]{1,0:T(8,128)(2,1)S(1)}, bf16[64,2048]{1,0:T(8,128)(2,1)S(1)}, u32[]{:S(2)}, u32[]{:S(2)}) collective-permute-start(bf16[64,2048]{1,0:T(8,128)(2,1)S(1)} %get-tuple-element.36), channel_id=1, source_target_pairs={{0,32},{32,64},{64,96},{96,0},{1,33},{33,65},{65,97},{97,1},{2,34}... | collective-permute-start | bytes 786440 | tf_op jit(solution)/shard_map/ppermute | solution.py:16
  82.4 6.4 %collective-permute-start.8 = (bf16[64,2048]{1,0:T(8,128)(2,1)S(1)}, bf16[64,2048]{1,0:T(8,128)(2,1)S(1)}, u32[]{:S(2)}, u32[]{:S(2)}) collective-permute-start(bf16[64,2048]{1,0:T(8,128)(2,1)S(1)} %get-tuple-element.37), channel_id=1, source_target_pairs={{0,96},{32,0},{64,32},{96,64},{1,97},{33,1},{65,33},{97,65},{2,98}... | collective-permute-start | bytes 786440 | tf_op jit(solution)/shard_map/ppermute | solution.py:16
  85.1 9.5 %collective-permute-start.10 = (bf16[64,2048]{1,0:T(8,128)(2,1)S(1)}, bf16[64,2048]{1,0:T(8,128)(2,1)S(1)}, u32[]{:S(2)}, u32[]{:S(2)}) collective-permute-start(bf16[64,2048]{1,0:T(8,128)(2,1)S(1)} %slice.91), channel_id=1, source_target_pairs={{0,32},{32,64},{64,96},{96,0},{1,33},{33,65},{65,97},{97,1},{2,34}... | collective-permute-start | bytes 786440 | tf_op jit(solution)/shard_map/ppermute | solution.py:16
  85.2 9.4 %collective-permute-start.11 = (bf16[64,2048]{1,0:T(8,128)(2,1)S(1)}, bf16[64,2048]{1,0:T(8,128)(2,1)S(1)}, u32[]{:S(2)}, u32[]{:S(2)}) collective-permute-start(bf16[64,2048]{1,0:T(8,128)(2,1)S(1)} %slice.92), channel_id=1, source_target_pairs={{0,96},{32,0},{64,32},{96,64},{1,97},{33,1},{65,33},{97,65},{2,98}... | collective-permute-start | bytes 786440 | tf_op jit(solution)/shard_map/ppermute | solution.py:16
  89.0 16.1 %collective-permute-start.9 = (bf16[128,2048]{1,0:T(8,128)(2,1)S(1)}, bf16[128,2048]{1,0:T(8,128)(2,1)S(1)}, u32[]{:S(2)}, u32[]{:S(2)}) collective-permute-start(bf16[128,2048]{1,0:T(8,128)(2,1)S(1)} %pad_maximum_fusion.1), channel_id=1, source_target_pairs={{0,96},{32,0},{64,32},{96,64},{1,97},{33,1},{65,33},{97,65},{2,98}... | collective-permute-start | bytes 1572872 | tf_op jit(solution)/shard_map/ppermute | solution.py:16
  91.7 13.3 %collective-permute-start.7 = (bf16[128,2048]{1,0:T(8,128)(2,1)S(1)}, bf16[128,2048]{1,0:T(8,128)(2,1)S(1)}, u32[]{:S(2)}, u32[]{:S(2)}) collective-permute-start(bf16[128,2048]{1,0:T(8,128)(2,1)S(1)} %pad_maximum_fusion), channel_id=1, source_target_pairs={{0,32},{32,64},{64,96},{96,0},{1,33},{33,65},{65,97},{97,1},{2,34}... | collective-permute-start | bytes 1572872 | tf_op jit(solution)/shard_map/ppermute | solution.py:16
  94.7 1.3 copy-start.5
  96.0 3.5 %copy-start.9 = (bf16[1,2048,1024]{2,1,0:T(8,128)(2,1)S(1)}, bf16[1,2048,1024]{2,1,0:T(8,128)(2,1)}, u32[]{:S(2)}) copy-start(bf16[1,2048,1024]{2,1,0:T(8,128)(2,1)} %param.10) | copy-start | bytes 12582916
  99.5 2.4 %copy-start.12 = (bf16[512,1024]{1,0:T(8,128)(2,1)}, bf16[512,1024]{1,0:T(8,128)(2,1)S(1)}, u32[]{:S(2)}) copy-start(bf16[512,1024]{1,0:T(8,128)(2,1)S(1)} %fusion.19) | copy-start | bytes 3145732
  101.9 3.7 %copy-start.3 = (f32[512,2048]{1,0:T(8,128)}, f32[512,2048]{1,0:T(8,128)S(1)}, u32[]{:S(2)}) copy-start(f32[512,2048]{1,0:T(8,128)S(1)} %fusion.4) | copy-start | bytes 12582916
  105.7 13.9 %collective-permute-start.12 = (bf16[64,2048]{1,0:T(8,128)(2,1)S(1)}, bf16[64,2048]{1,0:T(8,128)(2,1)S(1)}, u32[]{:S(2)}, u32[]{:S(2)}) collective-permute-start(bf16[64,2048]{1,0:T(8,128)(2,1)S(1)} %get-tuple-element.32), channel_id=1, source_target_pairs={{0,32},{32,64},{64,96},{96,0},{1,33},{33,65},{65,97},{97,1},{2,34}... | collective-permute-start | bytes 786440 | tf_op jit(solution)/shard_map/ppermute | solution.py:16
  106.8 12.8 %collective-permute-start.14 = (bf16[64,2048]{1,0:T(8,128)(2,1)S(1)}, bf16[64,2048]{1,0:T(8,128)(2,1)}, u32[]{:S(2)}, u32[]{:S(2)}) collective-permute-start(bf16[64,2048]{1,0:T(8,128)(2,1)S(1)} %get-tuple-element.33), channel_id=1, source_target_pairs={{0,96},{32,0},{64,32},{96,64},{1,97},{33,1},{65,33},{97,65},{2,98}... | collective-permute-start | bytes 786440 | tf_op jit(solution)/shard_map/ppermute | solution.py:16
  110.6 29.1 %all-to-all-start.3 = ((bf16[32,8,2048]{2,1,0:T(8,128)(2,1)}), bf16[32,8,2048]{2,1,0:T(8,128)(2,1)S(1)}, u32[]{:S(2)}, u32[]{:S(2)}) async-start(bf16[32,8,2048]{2,1,0:T(8,128)(2,1)} %fusion.10), calls=%async_computation.3 | async-start | bytes 2097152 | tf_op jit(solution)/shard_map/all_to_all | solution.py:46
  121.1 13.4 %collective-permute-start.15 = (bf16[128,2048]{1,0:T(8,128)(2,1)S(1)}, bf16[128,2048]{1,0:T(8,128)(2,1)S(1)}, u32[]{:S(2)}, u32[]{:S(2)}) collective-permute-start(bf16[128,2048]{1,0:T(8,128)(2,1)S(1)} %pad_maximum_fusion.3), channel_id=1, source_target_pairs={{0,96},{32,0},{64,32},{96,64},{1,97},{33,1},{65,33},{97,65},{2,98}... | collective-permute-start | bytes 1572872 | tf_op jit(solution)/shard_map/ppermute | solution.py:16
  122.8 14.3 %collective-permute-start.13 = (bf16[128,2048]{1,0:T(8,128)(2,1)S(1)}, bf16[128,2048]{1,0:T(8,128)(2,1)S(1)}, u32[]{:S(2)}, u32[]{:S(2)}) collective-permute-start(bf16[128,2048]{1,0:T(8,128)(2,1)S(1)} %pad_maximum_fusion.2), channel_id=1, source_target_pairs={{0,32},{32,64},{64,96},{96,0},{1,33},{33,65},{65,97},{97,1},{2,34}... | collective-permute-start | bytes 1572872 | tf_op jit(solution)/shard_map/ppermute | solution.py:16
  139.7 25.6 %all-to-all-start.4 = ((bf16[32,8,2048]{2,1,0:T(8,128)(2,1)}), bf16[32,8,2048]{2,1,0:T(8,128)(2,1)S(1)}, u32[]{:S(2)}, u32[]{:S(2)}) async-start(bf16[32,8,2048]{2,1,0:T(8,128)(2,1)} %fusion.11), calls=%async_computation.4 | async-start | bytes 2097152 | tf_op jit(solution)/shard_map/all_to_all | solution.py:46
  148.1 6.4 %copy-start.6 = (bf16[512,2048]{1,0:T(8,128)(2,1)S(1)}, bf16[512,2048]{1,0:T(8,128)(2,1)}, u32[]{:S(2)}) copy-start(bf16[512,2048]{1,0:T(8,128)(2,1)} %copy-done.5) | copy-start | bytes 6291460
  148.1 6.4 %copy-start.11 = (f32[512,1024]{1,0:T(8,128)S(1)}, f32[512,1024]{1,0:T(8,128)}, u32[]{:S(2)}) copy-start(f32[512,1024]{1,0:T(8,128)} %copy-done.10) | copy-start | bytes 6291460

commit v3 on v2

--- a/solution.py
+++ b/solution.py
@@ -40,6 +40,25 @@
     from_below = shifted(above, 1)
     from_above = shifted(below, -1)
     return own + from_below.astype(F32) + from_above.astype(F32)
+
+
+def added(first, second):
+    return first.astype(F32) + second.astype(F32)
+
+
+def joined_sum(parts):
+    own, below, above, far = jnp.split(parts, 4, axis=0)
+    half = own.shape[0] // 2
+    up = shifted(jnp.concatenate([far[:half], above[half:]], axis=0), 1)
+    down = shifted(jnp.concatenate([far[half:], below[:half]], axis=0), -1)
+    merged_upper = added(above[:half], up[:half]).astype(BF16)
+    merged_lower = added(below[half:], down[:half]).astype(BF16)
+    merged_upper, merged_lower = lax.optimization_barrier((merged_upper, merged_lower))
+    merged_upper = shifted(merged_upper, 1)
+    merged_lower = shifted(merged_lower, -1)
+    upper = added(own[:half], down[half:]) + merged_upper.astype(F32)
+    lower = added(own[half:], up[half:]) + merged_lower.astype(F32)
+    return jnp.concatenate([upper, lower], axis=0)
 
 
 def swap(array):
@@ -95,8 +114,10 @@
     def unslot(rows):
         return lax.dot_general(place, rows, (((0,), (0,)), ((), ())), preferred_element_type=F32)
 
-    def back(rows):
-        placed = jnp.dot(place, rows, preferred_element_type=F32).astype(BF16)
+    def put(rows):
+        return jnp.dot(place, rows, preferred_element_type=F32).astype(BF16)
+
+    def back(placed):
         came = swap(placed.reshape(experts, slot_size, width)).reshape(slots, width)
         return lax.dot_general(
             layout, came, (((0,), (0,)), ((), ())), preferred_element_type=F32
@@ -110,6 +131,8 @@
     packed_cot, came_in = lax.optimization_barrier((pack(out_grad), came_in))
     came_cot = swap(packed_cot).reshape(slots, width)
     inputs = ring_gather(unslot(came_in).astype(BF16))
+    inputs = list(inputs)
+    inputs[:2] = lax.optimization_barrier((inputs[0], inputs[1]))
     inputs = jnp.concatenate(inputs, axis=0)
     came_cot, inputs = lax.optimization_barrier((came_cot, inputs))
     dout_own = (own_gates * unslot(came_cot)).astype(BF16)
@@ -127,11 +150,13 @@
 
     dhid = lax.dot_general(dout, weight_out, (((1,), (1,)), ((), ())), preferred_element_type=F32)
     dact = gelu_back(dhid)[0].astype(BF16)
-    dpart = lax.dot_general(dact, weight_in, (((1,), (1,)), ((), ())), preferred_element_type=F32)
-    outputs, dpart = lax.optimization_barrier((outputs, dpart))
-    moe_out = back(outputs)
-    dinput = ring_sum(dpart).astype(BF16)
-    tokens_grad = back(dinput)
+    dpart = lax.dot_general(
+        dact, weight_in, (((1,), (1,)), ((), ())), preferred_element_type=F32
+    ).astype(BF16)
+    placed, dpart = lax.optimization_barrier((put(outputs), dpart))
+    moe_out = back(placed)
+    dinput = joined_sum(dpart).astype(BF16)
+    tokens_grad = back(put(dinput))
 
     grad_in = lax.dot_general(
         inputs, dact, (((0,), (0,)), ((), ())), preferred_element_type=F32

time: 167 us -> 162 us (0.970)
  waiting for transfers between devices: 62.5 us -> 55.4 us
  matrix products: 36.2 us -> 34.1 us
    ppermute x16, waiting for transfers between devices: 34.1 us -> 21.6 us  [shifted(): lax.ppermute(array, 'dp', [(i, (i + step) % count) for i in range(count)])]
    all_to_all x5, waiting for transfers between devices: 28.5 us -> 33.7 us  [swap(): lax.all_to_all(array, 'expert', split_axis=0, concat_axis=0, tiled=True)]
    unnamed x33 -> x34, local copies, waits for them, and re-layouts: 4.63 us -> 5.19 us
  transfers between devices with their start and end apart: 21 -> 21, of which waited for: 12 -> 11; matrix products, arithmetic and copies ran while one was open for 22% -> 24% of each run, Pallas kernels for 0% -> 0%
where the time goes in v3:
time: 162 us; the launch traced here: 161 us
  starting transfers between devices  59.2 us (37%)
  waiting for transfers between devices  55.4 us (34%)
  matrix products  34.1 us (21%)
  local copies, waits for them, and re-layouts  7.12 us (4%)
  other arithmetic  3.65 us (2%)
    all_to_all x5, starting transfers between devices, swap(): lax.all_to_all(array, 'expert', split_axis=0, concat_axis=0, tiled=True)  35.7 us
    all_to_all x5, waiting for transfers between devices, swap(): lax.all_to_all(array, 'expert', split_axis=0, concat_axis=0, tiled=True)  33.7 us
    ppermute x16, starting transfers between devices, shifted(): lax.ppermute(array, 'dp', [(i, (i + step) % count) for i in range(count)])  23.6 us
    ppermute x16, waiting for transfers between devices, shifted(): lax.ppermute(array, 'dp', [(i, (i + step) % count) for i in range(count)])  21.6 us
    dot_general x1, matrix products, on_device(): lax.dot_general(inputs, dact, (((0,), (0,)), ((), ())), preferred_element...  6.4 us
    unnamed x34, local copies, waits for them, and re-layouts  5.19 us
    dot_general x1, matrix products, on_device(): act = jnp.dot(inputs, weight_in, preferred_element_type=F32)  5.15 us
    dot_general x1, matrix products, on_device(): lax.dot_general(hidden, dout, (((0,), (0,)), ((), ())), preferred_element...  4.61 us
  transfers between devices with their start and end apart: 21, of which 11 were waited for; matrix products, arithmetic and copies ran while one was open for 24% of the time, Pallas kernels for 0%

profile of v3, /device:TPU:1, one launch (start us, length us, event | category | flops | bytes accessed | tf_op | source)
XLA Modules:
  0.0 161.5 jit_solution(12400356270047661323)
XLA Ops:
  0.7 0.7 copy-done.1
  1.4 0.9 shard_map.93
  2.3 9.6 %all-to-all-start = ((f32[32,8,128]{2,1,0:T(8,128)}), f32[32,8,128]{2,1,0:T(8,128)S(1)}, u32[]{:S(2)}, u32[]{:S(2)}) async-start(f32[32,8,128]{2,1,0:T(8,128)} %bitcast.1), calls=%async_computation | async-start | bytes 262144 | tf_op jit(solution)/shard_map/all_to_all | solution.py:65
  11.9 7.6 %all-to-all-done = f32[32,8,128]{2,1,0:T(8,128)S(1)} async-done(((f32[32,8,128]{2,1,0:T(8,128)}), f32[32,8,128]{2,1,0:T(8,128)S(1)}, u32[]{:S(2)}, u32[]{:S(2)}) %all-to-all-start) | async-done | bytes 131104 | tf_op jit(solution)/shard_map/all_to_all | solution.py:65
  19.7 1.4 fusion.12
  21.2 4.0 %all-to-all-start.1 = ((bf16[32,8,2048]{2,1,0:T(8,128)(2,1)}), bf16[32,8,2048]{2,1,0:T(8,128)(2,1)S(1)}, u32[]{:S(2)}, u32[]{:S(2)}) async-start(bf16[32,8,2048]{2,1,0:T(8,128)(2,1)} %fusion.12), calls=%async_computation.1 | async-start | bytes 2097152 | tf_op jit(solution)/shard_map/all_to_all | solution.py:65
  25.4 1.5 fusion.11
  26.9 15.6 %all-to-all-done.1 = bf16[32,8,2048]{2,1,0:T(8,128)(2,1)S(1)} async-done(((bf16[32,8,2048]{2,1,0:T(8,128)(2,1)}), bf16[32,8,2048]{2,1,0:T(8,128)(2,1)S(1)}, u32[]{:S(2)}, u32[]{:S(2)}) %all-to-all-start.1) | async-done | bytes 1048608 | tf_op jit(solution)/shard_map/all_to_all | solution.py:65
  42.8 1.3 collective-permute-start
  44.1 1.5 collective-permute-start.1
  45.6 4.5 %all-to-all-start.2 = ((bf16[32,8,2048]{2,1,0:T(8,128)(2,1)}), bf16[32,8,2048]{2,1,0:T(8,128)(2,1)S(1)}, u32[]{:S(2)}, u32[]{:S(2)}) async-start(bf16[32,8,2048]{2,1,0:T(8,128)(2,1)} %fusion.11), calls=%async_computation.2 | async-start | bytes 2097152 | tf_op jit(solution)/shard_map/all_to_all | solution.py:65
  50.1 7.1 %collective-permute-done = bf16[128,2048]{1,0:T(8,128)(2,1)S(1)} collective-permute-done((bf16[128,2048]{1,0:T(8,128)(2,1)S(1)}, bf16[128,2048]{1,0:T(8,128)(2,1)S(1)}, u32[]{:S(2)}, u32[]{:S(2)}) %collective-permute-start) | collective-permute-done | bytes 524320 | tf_op jit(solution)/shard_map/ppermute | solution.py:16
  57.2 0.8 constant_dynamic-update-slice_fusion.4
  58.2 1.0 slice.110
  59.2 2.6 %collective-permute-start.3 = (bf16[64,2048]{1,0:T(8,128)(2,1)S(1)}, bf16[64,2048]{1,0:T(8,128)(2,1)S(1)}, u32[]{:S(2)}, u32[]{:S(2)}) collective-permute-start(bf16[64,2048]{1,0:T(8,128)(2,1)S(1)} %slice.110), channel_id=1, source_target_pairs={{0,96},{32,0},{64,32},{96,64},{1,97},{33,1},{65,33},{97,65},{2,98}... | collective-permute-start | bytes 786440 | tf_op jit(solution)/shard_map/ppermute | solution.py:16
  61.8 0.8 constant_dynamic-update-slice_fusion.3
  62.7 1.9 %constant_dynamic-update-slice_fusion.2 = bf16[512,2048]{1,0:T(8,128)(2,1)} fusion(bf16[512,2048]{1,0:T(8,128)(2,1)} %constant_dynamic-update-slice_fusion.3, bf16[128,2048]{1,0:T(8,128)(2,1)} %collective-permute-done.1), kind=kLoop, calls=%fused_computation.74 | loop fusion | bytes 1048576
  64.5 1.4 collective-permute-done.2
  65.9 0.7 constant_dynamic-update-slice_fusion.1
  66.6 0.7 constant_dynamic-update-slice_fusion
  68.0 2.5 %collective-permute-start.5 = (bf16[128,2048]{1,0:T(8,128)(2,1)S(1)}, bf16[128,2048]{1,0:T(8,128)(2,1)S(1)}, u32[]{:S(2)}, u32[]{:S(2)}) collective-permute-start(bf16[128,2048]{1,0:T(8,128)(2,1)S(1)} %fusion.14), channel_id=1, source_target_pairs={{0,96},{32,0},{64,32},{96,64},{1,97},{33,1},{65,33},{97,65},{2,98}... | collective-permute-start | bytes 1572872 | tf_op jit(solution)/shard_map/ppermute | solution.py:16
  70.6 5.1 %fusion.6 = f32[512,1024]{1,0:T(8,128)S(1)} fusion(bf16[512,2048]{1,0:T(8,128)(2,1)} %constant_dynamic-update-slice_fusion, bf16[1,2048,1024]{2,1,0:T(8,128)(2,1)} %param.10), kind=kOutput, calls=%fused_computation.6 | convolution fusion | flops 2147483648 | bytes 8388608 | tf_op jit(solution)/shard_map/dot_general | solution.py:142
  75.8 2.5 %fusion.2 = f32[512,2048]{1,0:T(8,128)S(1)} fusion(bf16[1,1024,2048]{2,1,0:T(8,128)(2,1)S(1)} %copy-done.8, f32[512,1024]{1,0:T(8,128)S(1)} %fusion.6), kind=kOutput, calls=%fused_computation.2 | convolution fusion | flops 2152202240 | bytes 10485760 | tf_op jit(solution)/shard_map/dot_general | solution.py:145
  78.3 2.0 %collective-permute-done.4 = bf16[128,2048]{1,0:T(8,128)(2,1)S(1)} collective-permute-done((bf16[128,2048]{1,0:T(8,128)(2,1)S(1)}, bf16[128,2048]{1,0:T(8,128)(2,1)S(1)}, u32[]{:S(2)}, u32[]{:S(2)}) %collective-permute-start.4) | collective-permute-done | bytes 524320 | tf_op jit(solution)/shard_map/ppermute | solution.py:16
  80.7 0.6 collective-permute-start.6
  81.4 2.1 %collective-permute-start.8 = (bf16[64,2048]{1,0:T(8,128)(2,1)S(1)}, bf16[64,2048]{1,0:T(8,128)(2,1)S(1)}, u32[]{:S(2)}, u32[]{:S(2)}) collective-permute-start(bf16[64,2048]{1,0:T(8,128)(2,1)S(1)} %get-tuple-element.47), channel_id=1, source_target_pairs={{0,96},{32,0},{64,32},{96,64},{1,97},{33,1},{65,33},{97,65},{2,98}... | collective-permute-start | bytes 786440 | tf_op jit(solution)/shard_map/ppermute | solution.py:16
  83.7 2.7 %collective-permute-start.11 = (bf16[64,2048]{1,0:T(8,128)(2,1)S(1)}, bf16[64,2048]{1,0:T(8,128)(2,1)S(1)}, u32[]{:S(2)}, u32[]{:S(2)}) collective-permute-start(bf16[64,2048]{1,0:T(8,128)(2,1)S(1)} %slice.116), channel_id=1, source_target_pairs={{0,96},{32,0},{64,32},{96,64},{1,97},{33,1},{65,33},{97,65},{2,98}... | collective-permute-start | bytes 786440 | tf_op jit(solution)/shard_map/ppermute | solution.py:16
  86.5 0.8 collective-permute-done.6
  87.4 2.7 %collective-permute-start.9 = (bf16[128,2048]{1,0:T(8,128)(2,1)S(1)}, bf16[128,2048]{1,0:T(8,128)(2,1)S(1)}, u32[]{:S(2)}, u32[]{:S(2)}) collective-permute-start(bf16[128,2048]{1,0:T(8,128)(2,1)S(1)} %pad_maximum_fusion.1), channel_id=1, source_target_pairs={{0,96},{32,0},{64,32},{96,64},{1,97},{33,1},{65,33},{97,65},{2,98}... | collective-permute-start | bytes 1572872 | tf_op jit(solution)/shard_map/ppermute | solution.py:16
  90.5 2.0 %collective-permute-done.10 = bf16[64,2048]{1,0:T(8,128)(2,1)S(1)} collective-permute-done((bf16[64,2048]{1,0:T(8,128)(2,1)S(1)}, bf16[64,2048]{1,0:T(8,128)(2,1)S(1)}, u32[]{:S(2)}, u32[]{:S(2)}) %collective-permute-start.10) | collective-permute-done | bytes 262176 | tf_op jit(solution)/shard_map/ppermute | solution.py:16
  92.6 3.4 %fusion.21 = bf16[512,1024]{1,0:T(8,128)(2,1)S(1)} fusion(f32[512,1024]{1,0:T(8,128)S(1)} %fusion.6, bf16[512,2048]{1,0:T(8,128)(2,1)S(1)} %constant_dynamic-update-slice_fusion.5, bf16[1,1024,2048]{2,1,0:T(8,128)(2,1)S(1)} %copy-done.8), kind=kOutput, calls=%fused_computation.31 | convolution fusion | flops 2157969408 | bytes 9437184 | tf_op jit(solution)/shard_map/dot_general | solution.py:151
  96.1 2.4 %fusion.8 = bf16[512,2048]{1,0:T(8,128)(2,1)S(1)} fusion(bf16[512,1024]{1,0:T(8,128)(2,1)S(1)} %fusion.21, bf16[1,2048,1024]{2,1,0:T(8,128)(2,1)S(1)} %copy-done.9), kind=kOutput, calls=%fused_computation.12 | convolution fusion | flops 2148532224 | bytes 7340032 | tf_op jit(solution)/shard_map/dot_general | solution.py:153
  98.5 4.4 %collective-permute-done.9 = bf16[128,2048]{1,0:T(8,128)(2,1)S(1)} collective-permute-done((bf16[128,2048]{1,0:T(8,128)(2,1)S(1)}, bf16[128,2048]{1,0:T(8,128)(2,1)S(1)}, u32[]{:S(2)}, u32[]{:S(2)}) %collective-permute-start.9) | collective-permute-done | bytes 524320 | tf_op jit(solution)/shard_map/ppermute | solution.py:16
  102.9 1.5 convolution_convert_fusion.1
  104.5 3.5 %collective-permute-start.12 = (bf16[128,2048]{1,0:T(8,128)(2,1)S(1)}, bf16[128,2048]{1,0:T(8,128)(2,1)}, u32[]{:S(2)}, u32[]{:S(2)}) collective-permute-start(bf16[128,2048]{1,0:T(8,128)(2,1)S(1)} %pad_maximum_fusion.2), channel_id=1, source_target_pairs={{0,96},{32,0},{64,32},{96,64},{1,97},{33,1},{65,33},{97,65},{2,98}... | collective-permute-start | bytes 1572872 | tf_op jit(solution)/shard_map/ppermute | solution.py:16
  108.1 10.6 %all-to-all-start.3 = ((bf16[32,8,2048]{2,1,0:T(8,128)(2,1)}), bf16[32,8,2048]{2,1,0:T(8,128)(2,1)S(1)}, u32[]{:S(2)}, u32[]{:S(2)}) async-start(bf16[32,8,2048]{2,1,0:T(8,128)(2,1)} %bitcast.11), calls=%async_computation.3 | async-start | bytes 2097152 | tf_op jit(solution)/shard_map/all_to_all | solution.py:65
  118.7 1.3 add_convert_fusion.2
  120.1 3.0 %collective-permute-start.15 = (bf16[64,2048]{1,0:T(8,128)(2,1)S(1)}, bf16[64,2048]{1,0:T(8,128)(2,1)S(1)}, u32[]{:S(2)}, u32[]{:S(2)}) collective-permute-start(bf16[64,2048]{1,0:T(8,128)(2,1)S(1)} %get-tuple-element.35), channel_id=1, source_target_pairs={{0,96},{32,0},{64,32},{96,64},{1,97},{33,1},{65,33},{97,65},{2,98}... | collective-permute-start | bytes 786440 | tf_op jit(solution)/shard_map/ppermute | solution.py:16
  123.1 4.0 %collective-permute-done.14 = bf16[64,2048]{1,0:T(8,128)(2,1)S(1)} collective-permute-done((bf16[64,2048]{1,0:T(8,128)(2,1)S(1)}, bf16[64,2048]{1,0:T(8,128)(2,1)S(1)}, u32[]{:S(2)}, u32[]{:S(2)}) %collective-permute-start.14) | collective-permute-done | bytes 262176 | tf_op jit(solution)/shard_map/ppermute | solution.py:16
  127.1 1.4 add_convert_fusion.1
  128.5 1.4 fusion.13
  130.0 5.9 %all-to-all-done.3 = bf16[32,8,2048]{2,1,0:T(8,128)(2,1)S(1)} async-done(((bf16[32,8,2048]{2,1,0:T(8,128)(2,1)}), bf16[32,8,2048]{2,1,0:T(8,128)(2,1)S(1)}, u32[]{:S(2)}, u32[]{:S(2)}) %all-to-all-start.3) | async-done | bytes 1048608 | tf_op jit(solution)/shard_map/all_to_all | solution.py:65
  135.9 6.9 %all-to-all-start.4 = ((bf16[32,8,2048]{2,1,0:T(8,128)(2,1)}), bf16[32,8,2048]{2,1,0:T(8,128)(2,1)S(1)}, u32[]{:S(2)}, u32[]{:S(2)}) async-start(bf16[32,8,2048]{2,1,0:T(8,128)(2,1)} %fusion.13), calls=%async_computation.4 | async-start | bytes 2097152 | tf_op jit(solution)/shard_map/all_to_all | solution.py:65
  142.8 6.4 %convert_bitcast_fusion.1 = bf16[1,2048,1024]{2,1,0:T(8,128)(2,1)} fusion(bf16[512,2048]{1,0:T(8,128)(2,1)} %constant_dynamic-update-slice_fusion, bf16[512,1024]{1,0:T(8,128)(2,1)} %copy-done.12), kind=kOutput, calls=%fused_computation.9 | convolution fusion | flops 2149580800 | bytes 7340032 | tf_op jit(solution)/shard_map/dot_general | solution.py:161
  149.2 4.6 %convert_bitcast_fusion = bf16[1,1024,2048]{2,1,0:T(8,128)(2,1)} fusion(bf16[512,2048]{1,0:T(8,128)(2,1)S(1)} %copy-done.6, f32[512,1024]{1,0:T(8,128)S(1)} %copy-done.11), kind=kOutput, calls=%fused_computation.8 | convolution fusion | flops 2154299392 | bytes 8388608 | tf_op jit(solution)/shard_map/dot_general | solution.py:164
  153.8 1.5 convolution_convert_fusion.3
  155.4 4.6 %all-to-all-done.4 = bf16[32,8,2048]{2,1,0:T(8,128)(2,1)S(1)} async-done(((bf16[32,8,2048]{2,1,0:T(8,128)(2,1)}), bf16[32,8,2048]{2,1,0:T(8,128)(2,1)S(1)}, u32[]{:S(2)}, u32[]{:S(2)}) %all-to-all-start.4) | async-done | bytes 1048608 | tf_op jit(solution)/shard_map/all_to_all | solution.py:65
  160.0 1.5 convolution_convert_fusion.2
  (64 shorter events, 3.0 us)
Async XLA Ops:
  0.6 19.1 %copy-start = (bf16[256,2048]{1,0:T(8,128)(2,1)S(1)}, bf16[256,2048]{1,0:T(8,128)(2,1)}, u32[]{:S(2)}) copy-start(bf16[256,2048]{1,0:T(8,128)(2,1)} %param.6) | copy-start | bytes 3145732
  0.6 0.7 copy-start.1
  2.3 17.2 %all-to-all-start = ((f32[32,8,128]{2,1,0:T(8,128)}), f32[32,8,128]{2,1,0:T(8,128)S(1)}, u32[]{:S(2)}, u32[]{:S(2)}) async-start(f32[32,8,128]{2,1,0:T(8,128)} %bitcast.1), calls=%async_computation | async-start | bytes 262144 | tf_op jit(solution)/shard_map/all_to_all | solution.py:65
  19.7 5.5 %copy-start.2 = (s32[1,1,128]{2,1,0:T(1,128)S(1)}, s32[1,1,128]{2,1,0:T(1,128)}, u32[]{:S(2)}) copy-start(s32[1,1,128]{2,1,0:T(1,128)} %param.8) | copy-start | bytes 1540
  19.7 5.7 %copy-start.4 = (bf16[256,2048]{1,0:T(8,128)(2,1)S(1)}, bf16[256,2048]{1,0:T(8,128)(2,1)}, u32[]{:S(2)}) copy-start(bf16[256,2048]{1,0:T(8,128)(2,1)} %param.7) | copy-start | bytes 3145732
  21.2 21.3 %all-to-all-start.1 = ((bf16[32,8,2048]{2,1,0:T(8,128)(2,1)}), bf16[32,8,2048]{2,1,0:T(8,128)(2,1)S(1)}, u32[]{:S(2)}, u32[]{:S(2)}) async-start(bf16[32,8,2048]{2,1,0:T(8,128)(2,1)} %fusion.12), calls=%async_computation.1 | async-start | bytes 2097152 | tf_op jit(solution)/shard_map/all_to_all | solution.py:65
  42.8 14.4 %collective-permute-start = (bf16[128,2048]{1,0:T(8,128)(2,1)S(1)}, bf16[128,2048]{1,0:T(8,128)(2,1)S(1)}, u32[]{:S(2)}, u32[]{:S(2)}) collective-permute-start(bf16[128,2048]{1,0:T(8,128)(2,1)S(1)} %convolution_convert_fusion.6), channel_id=1, source_target_pairs={{0,32},{32,64},{64,96},{96,0},{1,33},{33,65},{65,97},{97,1},{2,34}... | collective-permute-start | bytes 1572872 | tf_op jit(solution)/shard_map/ppermute | solution.py:16
  44.1 14.1 %collective-permute-start.1 = (bf16[128,2048]{1,0:T(8,128)(2,1)S(1)}, bf16[128,2048]{1,0:T(8,128)(2,1)}, u32[]{:S(2)}, u32[]{:S(2)}) collective-permute-start(bf16[128,2048]{1,0:T(8,128)(2,1)S(1)} %convolution_convert_fusion.6), channel_id=1, source_target_pairs={{0,96},{32,0},{64,32},{96,64},{1,97},{33,1},{65,33},{97,65},{2,98}... | collective-permute-start | bytes 1572872 | tf_op jit(solution)/shard_map/ppermute | solution.py:16
  45.6 21.8 %all-to-all-start.2 = ((bf16[32,8,2048]{2,1,0:T(8,128)(2,1)}), bf16[32,8,2048]{2,1,0:T(8,128)(2,1)S(1)}, u32[]{:S(2)}, u32[]{:S(2)}) async-start(bf16[32,8,2048]{2,1,0:T(8,128)(2,1)} %fusion.11), calls=%async_computation.2 | async-start | bytes 2097152 | tf_op jit(solution)/shard_map/all_to_all | solution.py:65
  58.0 9.4 %copy-start.7 = (f32[1,1,128]{2,1,0:T(1,128)S(1)}, f32[1,1,128]{2,1,0:T(1,128)}, u32[]{:S(2)}) copy-start(f32[1,1,128]{2,1,0:T(1,128)} %param.9) | copy-start | bytes 1540
  58.0 7.9 %collective-permute-start.2 = (bf16[64,2048]{1,0:T(8,128)(2,1)S(1)}, bf16[64,2048]{1,0:T(8,128)(2,1)S(1)}, u32[]{:S(2)}, u32[]{:S(2)}) collective-permute-start(bf16[64,2048]{1,0:T(8,128)(2,1)S(1)} %slice.109), channel_id=1, source_target_pairs={{0,32},{32,64},{64,96},{96,0},{1,33},{33,65},{65,97},{97,1},{2,34}... | collective-permute-start | bytes 786440 | tf_op jit(solution)/shard_map/ppermute | solution.py:16
  59.2 7.4 %collective-permute-start.3 = (bf16[64,2048]{1,0:T(8,128)(2,1)S(1)}, bf16[64,2048]{1,0:T(8,128)(2,1)S(1)}, u32[]{:S(2)}, u32[]{:S(2)}) collective-permute-start(bf16[64,2048]{1,0:T(8,128)(2,1)S(1)} %slice.110), channel_id=1, source_target_pairs={{0,96},{32,0},{64,32},{96,64},{1,97},{33,1},{65,33},{97,65},{2,98}... | collective-permute-start | bytes 786440 | tf_op jit(solution)/shard_map/ppermute | solution.py:16
  67.7 8.0 %copy-start.8 = (bf16[1,1024,2048]{2,1,0:T(8,128)(2,1)S(1)}, bf16[1,1024,2048]{2,1,0:T(8,128)(2,1)}, u32[]{:S(2)}) copy-start(bf16[1,1024,2048]{2,1,0:T(8,128)(2,1)} %param.11) | copy-start | bytes 12582916
  67.8 12.6 %collective-permute-start.4 = (bf16[128,2048]{1,0:T(8,128)(2,1)S(1)}, bf16[128,2048]{1,0:T(8,128)(2,1)S(1)}, u32[]{:S(2)}, u32[]{:S(2)}) collective-permute-start(bf16[128,2048]{1,0:T(8,128)(2,1)S(1)} %fusion.14), channel_id=1, source_target_pairs={{0,32},{32,64},{64,96},{96,0},{1,33},{33,65},{65,97},{97,1},{2,34}... | collective-permute-start | bytes 1572872 | tf_op jit(solution)/shard_map/ppermute | solution.py:16
  68.0 12.3 %collective-permute-start.5 = (bf16[128,2048]{1,0:T(8,128)(2,1)S(1)}, bf16[128,2048]{1,0:T(8,128)(2,1)S(1)}, u32[]{:S(2)}, u32[]{:S(2)}) collective-permute-start(bf16[128,2048]{1,0:T(8,128)(2,1)S(1)} %fusion.14), channel_id=1, source_target_pairs={{0,96},{32,0},{64,32},{96,64},{1,97},{33,1},{65,33},{97,65},{2,98}... | collective-permute-start | bytes 1572872 | tf_op jit(solution)/shard_map/ppermute | solution.py:16
  75.8 16.8 %copy-start.10 = (f32[512,1024]{1,0:T(8,128)}, f32[512,1024]{1,0:T(8,128)S(1)}, u32[]{:S(2)}) copy-start(f32[512,1024]{1,0:T(8,128)S(1)} %fusion.6) | copy-start | bytes 6291460
  80.7 6.5 %collective-permute-start.6 = (bf16[64,2048]{1,0:T(8,128)(2,1)S(1)}, bf16[64,2048]{1,0:T(8,128)(2,1)S(1)}, u32[]{:S(2)}, u32[]{:S(2)}) collective-permute-start(bf16[64,2048]{1,0:T(8,128)(2,1)S(1)} %get-tuple-element.46), channel_id=1, source_target_pairs={{0,32},{32,64},{64,96},{96,0},{1,33},{33,65},{65,97},{97,1},{2,34}... | collective-permute-start | bytes 786440 | tf_op jit(solution)/shard_map/ppermute | solution.py:16
  81.4 5.9 %collective-permute-start.8 = (bf16[64,2048]{1,0:T(8,128)(2,1)S(1)}, bf16[64,2048]{1,0:T(8,128)(2,1)S(1)}, u32[]{:S(2)}, u32[]{:S(2)}) collective-permute-start(bf16[64,2048]{1,0:T(8,128)(2,1)S(1)} %get-tuple-element.47), channel_id=1, source_target_pairs={{0,96},{32,0},{64,32},{96,64},{1,97},{33,1},{65,33},{97,65},{2,98}... | collective-permute-start | bytes 786440 | tf_op jit(solution)/shard_map/ppermute | solution.py:16
  83.6 8.9 %collective-permute-start.10 = (bf16[64,2048]{1,0:T(8,128)(2,1)S(1)}, bf16[64,2048]{1,0:T(8,128)(2,1)S(1)}, u32[]{:S(2)}, u32[]{:S(2)}) collective-permute-start(bf16[64,2048]{1,0:T(8,128)(2,1)S(1)} %slice.115), channel_id=1, source_target_pairs={{0,32},{32,64},{64,96},{96,0},{1,33},{33,65},{65,97},{97,1},{2,34}... | collective-permute-start | bytes 786440 | tf_op jit(solution)/shard_map/ppermute | solution.py:16
  83.7 8.8 %collective-permute-start.11 = (bf16[64,2048]{1,0:T(8,128)(2,1)S(1)}, bf16[64,2048]{1,0:T(8,128)(2,1)S(1)}, u32[]{:S(2)}, u32[]{:S(2)}) collective-permute-start(bf16[64,2048]{1,0:T(8,128)(2,1)S(1)} %slice.116), channel_id=1, source_target_pairs={{0,96},{32,0},{64,32},{96,64},{1,97},{33,1},{65,33},{97,65},{2,98}... | collective-permute-start | bytes 786440 | tf_op jit(solution)/shard_map/ppermute | solution.py:16
  87.4 15.4 %collective-permute-start.9 = (bf16[128,2048]{1,0:T(8,128)(2,1)S(1)}, bf16[128,2048]{1,0:T(8,128)(2,1)S(1)}, u32[]{:S(2)}, u32[]{:S(2)}) collective-permute-start(bf16[128,2048]{1,0:T(8,128)(2,1)S(1)} %pad_maximum_fusion.1), channel_id=1, source_target_pairs={{0,96},{32,0},{64,32},{96,64},{1,97},{33,1},{65,33},{97,65},{2,98}... | collective-permute-start | bytes 1572872 | tf_op jit(solution)/shard_map/ppermute | solution.py:16
  90.2 12.7 %collective-permute-start.7 = (bf16[128,2048]{1,0:T(8,128)(2,1)S(1)}, bf16[128,2048]{1,0:T(8,128)(2,1)S(1)}, u32[]{:S(2)}, u32[]{:S(2)}) collective-permute-start(bf16[128,2048]{1,0:T(8,128)(2,1)S(1)} %pad_maximum_fusion), channel_id=1, source_target_pairs={{0,32},{32,64},{64,96},{96,0},{1,33},{33,65},{65,97},{97,1},{2,34}... | collective-permute-start | bytes 1572872 | tf_op jit(solution)/shard_map/ppermute | solution.py:16
  92.6 3.5 %copy-start.5 = (bf16[512,2048]{1,0:T(8,128)(2,1)}, bf16[512,2048]{1,0:T(8,128)(2,1)S(1)}, u32[]{:S(2)}) copy-start(bf16[512,2048]{1,0:T(8,128)(2,1)S(1)} %constant_dynamic-update-slice_fusion.5) | copy-start | bytes 6291460
  92.6 3.5 %copy-start.9 = (bf16[1,2048,1024]{2,1,0:T(8,128)(2,1)S(1)}, bf16[1,2048,1024]{2,1,0:T(8,128)(2,1)}, u32[]{:S(2)}) copy-start(bf16[1,2048,1024]{2,1,0:T(8,128)(2,1)} %param.10) | copy-start | bytes 12582916
  96.1 2.4 %copy-start.12 = (bf16[512,1024]{1,0:T(8,128)(2,1)}, bf16[512,1024]{1,0:T(8,128)(2,1)S(1)}, u32[]{:S(2)}) copy-start(bf16[512,1024]{1,0:T(8,128)(2,1)S(1)} %fusion.21) | copy-start | bytes 3145732
  98.5 6.0 %copy-start.3 = (bf16[512,2048]{1,0:T(8,128)(2,1)}, bf16[512,2048]{1,0:T(8,128)(2,1)S(1)}, u32[]{:S(2)}) copy-start(bf16[512,2048]{1,0:T(8,128)(2,1)S(1)} %fusion.8) | copy-start | bytes 6291460
  104.5 14.2 %collective-permute-start.12 = (bf16[128,2048]{1,0:T(8,128)(2,1)S(1)}, bf16[128,2048]{1,0:T(8,128)(2,1)}, u32[]{:S(2)}, u32[]{:S(2)}) collective-permute-start(bf16[128,2048]{1,0:T(8,128)(2,1)S(1)} %pad_maximum_fusion.2), channel_id=1, source_target_pairs={{0,96},{32,0},{64,32},{96,64},{1,97},{33,1},{65,33},{97,65},{2,98}... | collective-permute-start | bytes 1572872 | tf_op jit(solution)/shard_map/ppermute | solution.py:16
  108.0 10.7 %collective-permute-start.13 = (bf16[128,2048]{1,0:T(8,128)(2,1)S(1)}, bf16[128,2048]{1,0:T(8,128)(2,1)}, u32[]{:S(2)}, u32[]{:S(2)}) collective-permute-start(bf16[128,2048]{1,0:T(8,128)(2,1)S(1)} %pad_maximum_fusion.3), channel_id=1, source_target_pairs={{0,32},{32,64},{64,96},{96,0},{1,33},{33,65},{65,97},{97,1},{2,34}... | collective-permute-start | bytes 1572872 | tf_op jit(solution)/shard_map/ppermute | solution.py:16
  108.1 27.8 %all-to-all-start.3 = ((bf16[32,8,2048]{2,1,0:T(8,128)(2,1)}), bf16[32,8,2048]{2,1,0:T(8,128)(2,1)S(1)}, u32[]{:S(2)}, u32[]{:S(2)}) async-start(bf16[32,8,2048]{2,1,0:T(8,128)(2,1)} %bitcast.11), calls=%async_computation.3 | async-start | bytes 2097152 | tf_op jit(solution)/shard_map/all_to_all | solution.py:65
  120.0 7.1 %collective-permute-start.14 = (bf16[64,2048]{1,0:T(8,128)(2,1)S(1)}, bf16[64,2048]{1,0:T(8,128)(2,1)S(1)}, u32[]{:S(2)}, u32[]{:S(2)}) collective-permute-start(bf16[64,2048]{1,0:T(8,128)(2,1)S(1)} %get-tuple-element.34), channel_id=1, source_target_pairs={{0,32},{32,64},{64,96},{96,0},{1,33},{33,65},{65,97},{97,1},{2,34}... | collective-permute-start | bytes 786440 | tf_op jit(solution)/shard_map/ppermute | solution.py:16
  120.1 7.0 %collective-permute-start.15 = (bf16[64,2048]{1,0:T(8,128)(2,1)S(1)}, bf16[64,2048]{1,0:T(8,128)(2,1)S(1)}, u32[]{:S(2)}, u32[]{:S(2)}) collective-permute-start(bf16[64,2048]{1,0:T(8,128)(2,1)S(1)} %get-tuple-element.35), channel_id=1, source_target_pairs={{0,96},{32,0},{64,32},{96,64},{1,97},{33,1},{65,33},{97,65},{2,98}... | collective-permute-start | bytes 786440 | tf_op jit(solution)/shard_map/ppermute | solution.py:16
  135.9 24.1 %all-to-all-start.4 = ((bf16[32,8,2048]{2,1,0:T(8,128)(2,1)}), bf16[32,8,2048]{2,1,0:T(8,128)(2,1)S(1)}, u32[]{:S(2)}, u32[]{:S(2)}) async-start(bf16[32,8,2048]{2,1,0:T(8,128)(2,1)} %fusion.13), calls=%async_computation.4 | async-start | bytes 2097152 | tf_op jit(solution)/shard_map/all_to_all | solution.py:65
  142.8 6.4 %copy-start.6 = (bf16[512,2048]{1,0:T(8,128)(2,1)S(1)}, bf16[512,2048]{1,0:T(8,128)(2,1)}, u32[]{:S(2)}) copy-start(bf16[512,2048]{1,0:T(8,128)(2,1)} %copy-done.5) | copy-start | bytes 6291460
  142.8 6.4 %copy-start.11 = (f32[512,1024]{1,0:T(8,128)S(1)}, f32[512,1024]{1,0:T(8,128)}, u32[]{:S(2)}) copy-start(f32[512,1024]{1,0:T(8,128)} %copy-done.10) | copy-start | bytes 6291460

commit v4 on v3

--- a/solution.py
+++ b/solution.py
@@ -37,6 +37,7 @@
     below = jnp.concatenate(
         [below[:half].astype(BF16), (below[half:] + to_below.astype(F32)).astype(BF16)], axis=0
     )
+    above, below = lax.optimization_barrier((above, below))
     from_below = shifted(above, 1)
     from_above = shifted(below, -1)
     return own + from_below.astype(F32) + from_above.astype(F32)

time: 162 us -> 162 us (level)
  starting transfers between devices: 59.2 us -> 54.4 us
  waiting for transfers between devices: 55.4 us -> 60 us
    ppermute x16, waiting for transfers between devices: 21.6 us -> 26 us  [shifted(): lax.ppermute(array, 'dp', [(i, (i + step) % count) for i in range(count)])]
    ppermute x16, starting transfers between devices: 23.6 us -> 19.6 us  [shifted(): lax.ppermute(array, 'dp', [(i, (i + step) % count) for i in range(count)])]
  transfers between devices with their start and end apart: 21 -> 21, of which waited for: 11 -> 13; matrix products, arithmetic and copies ran while one was open for 24% -> 24% of each run, Pallas kernels for 0% -> 0%
where the time goes in v4:
time: 162 us; the launch traced here: 161 us
  waiting for transfers between devices  60 us (37%)
  starting transfers between devices  54.4 us (34%)
  matrix products  34.1 us (21%)
  local copies, waits for them, and re-layouts  7.11 us (4%)
  other arithmetic  3.68 us (2%)
    all_to_all x5, starting transfers between devices, swap(): lax.all_to_all(array, 'expert', split_axis=0, concat_axis=0, tiled=True)  34.8 us
    all_to_all x5, waiting for transfers between devices, swap(): lax.all_to_all(array, 'expert', split_axis=0, concat_axis=0, tiled=True)  34 us
    ppermute x16, waiting for transfers between devices, shifted(): lax.ppermute(array, 'dp', [(i, (i + step) % count) for i in range(count)])  26 us
    ppermute x16, starting transfers between devices, shifted(): lax.ppermute(array, 'dp', [(i, (i + step) % count) for i in range(count)])  19.6 us
    dot_general x1, matrix products, on_device(): lax.dot_general(inputs, dact, (((0,), (0,)), ((), ())), preferred_element...  6.4 us
    unnamed x34, local copies, waits for them, and re-layouts  5.19 us
    dot_general x1, matrix products, on_device(): act = jnp.dot(inputs, weight_in, preferred_element_type=F32)  5.15 us
    dot_general x1, matrix products, on_device(): lax.dot_general(hidden, dout, (((0,), (0,)), ((), ())), preferred_element...  4.61 us
  transfers between devices with their start and end apart: 21, of which 13 were waited for; matrix products, arithmetic and copies ran while one was open for 24% of the time, Pallas kernels for 0%

profile of v4, /device:TPU:1, one launch (start us, length us, event | category | flops | bytes accessed | tf_op | source)
XLA Modules:
  0.0 161.3 jit_solution(8855231833499972895)
XLA Ops:
  0.7 0.7 copy-done.1
  1.4 0.9 shard_map.93
  2.3 9.6 %all-to-all-start = ((f32[32,8,128]{2,1,0:T(8,128)}), f32[32,8,128]{2,1,0:T(8,128)S(1)}, u32[]{:S(2)}, u32[]{:S(2)}) async-start(f32[32,8,128]{2,1,0:T(8,128)} %bitcast.1), calls=%async_computation | async-start | bytes 262144 | tf_op jit(solution)/shard_map/all_to_all | solution.py:66
  11.9 7.6 %all-to-all-done = f32[32,8,128]{2,1,0:T(8,128)S(1)} async-done(((f32[32,8,128]{2,1,0:T(8,128)}), f32[32,8,128]{2,1,0:T(8,128)S(1)}, u32[]{:S(2)}, u32[]{:S(2)}) %all-to-all-start) | async-done | bytes 131104 | tf_op jit(solution)/shard_map/all_to_all | solution.py:66
  19.7 1.4 fusion.12
  21.2 4.0 %all-to-all-start.1 = ((bf16[32,8,2048]{2,1,0:T(8,128)(2,1)}), bf16[32,8,2048]{2,1,0:T(8,128)(2,1)S(1)}, u32[]{:S(2)}, u32[]{:S(2)}) async-start(bf16[32,8,2048]{2,1,0:T(8,128)(2,1)} %fusion.12), calls=%async_computation.1 | async-start | bytes 2097152 | tf_op jit(solution)/shard_map/all_to_all | solution.py:66
  25.4 1.5 fusion.11
  26.9 15.6 %all-to-all-done.1 = bf16[32,8,2048]{2,1,0:T(8,128)(2,1)S(1)} async-done(((bf16[32,8,2048]{2,1,0:T(8,128)(2,1)}), bf16[32,8,2048]{2,1,0:T(8,128)(2,1)S(1)}, u32[]{:S(2)}, u32[]{:S(2)}) %all-to-all-start.1) | async-done | bytes 1048608 | tf_op jit(solution)/shard_map/all_to_all | solution.py:66
  42.8 1.3 collective-permute-start
  44.1 1.5 collective-permute-start.1
  45.6 4.5 %all-to-all-start.2 = ((bf16[32,8,2048]{2,1,0:T(8,128)(2,1)}), bf16[32,8,2048]{2,1,0:T(8,128)(2,1)S(1)}, u32[]{:S(2)}, u32[]{:S(2)}) async-start(bf16[32,8,2048]{2,1,0:T(8,128)(2,1)} %fusion.11), calls=%async_computation.2 | async-start | bytes 2097152 | tf_op jit(solution)/shard_map/all_to_all | solution.py:66
  50.1 7.1 %collective-permute-done = bf16[128,2048]{1,0:T(8,128)(2,1)S(1)} collective-permute-done((bf16[128,2048]{1,0:T(8,128)(2,1)S(1)}, bf16[128,2048]{1,0:T(8,128)(2,1)S(1)}, u32[]{:S(2)}, u32[]{:S(2)}) %collective-permute-start) | collective-permute-done | bytes 524320 | tf_op jit(solution)/shard_map/ppermute | solution.py:16
  57.2 0.8 constant_dynamic-update-slice_fusion.4
  58.2 1.0 slice.110
  59.2 2.6 %collective-permute-start.3 = (bf16[64,2048]{1,0:T(8,128)(2,1)S(1)}, bf16[64,2048]{1,0:T(8,128)(2,1)S(1)}, u32[]{:S(2)}, u32[]{:S(2)}) collective-permute-start(bf16[64,2048]{1,0:T(8,128)(2,1)S(1)} %slice.110), channel_id=1, source_target_pairs={{0,96},{32,0},{64,32},{96,64},{1,97},{33,1},{65,33},{97,65},{2,98}... | collective-permute-start | bytes 786440 | tf_op jit(solution)/shard_map/ppermute | solution.py:16
  61.8 0.8 constant_dynamic-update-slice_fusion.3
  62.7 1.9 %constant_dynamic-update-slice_fusion.2 = bf16[512,2048]{1,0:T(8,128)(2,1)} fusion(bf16[512,2048]{1,0:T(8,128)(2,1)} %constant_dynamic-update-slice_fusion.3, bf16[128,2048]{1,0:T(8,128)(2,1)} %collective-permute-done.1), kind=kLoop, calls=%fused_computation.74 | loop fusion | bytes 1048576
  64.5 1.4 collective-permute-done.2
  65.9 0.7 constant_dynamic-update-slice_fusion.1
  66.6 0.7 constant_dynamic-update-slice_fusion
  68.0 2.5 %collective-permute-start.5 = (bf16[128,2048]{1,0:T(8,128)(2,1)S(1)}, bf16[128,2048]{1,0:T(8,128)(2,1)S(1)}, u32[]{:S(2)}, u32[]{:S(2)}) collective-permute-start(bf16[128,2048]{1,0:T(8,128)(2,1)S(1)} %fusion.14), channel_id=1, source_target_pairs={{0,96},{32,0},{64,32},{96,64},{1,97},{33,1},{65,33},{97,65},{2,98}... | collective-permute-start | bytes 1572872 | tf_op jit(solution)/shard_map/ppermute | solution.py:16
  70.6 5.1 %fusion.6 = f32[512,1024]{1,0:T(8,128)S(1)} fusion(bf16[512,2048]{1,0:T(8,128)(2,1)} %constant_dynamic-update-slice_fusion, bf16[1,2048,1024]{2,1,0:T(8,128)(2,1)} %param.10), kind=kOutput, calls=%fused_computation.6 | convolution fusion | flops 2147483648 | bytes 8388608 | tf_op jit(solution)/shard_map/dot_general | solution.py:143
  75.8 2.5 %fusion.2 = f32[512,2048]{1,0:T(8,128)S(1)} fusion(bf16[1,1024,2048]{2,1,0:T(8,128)(2,1)S(1)} %copy-done.8, f32[512,1024]{1,0:T(8,128)S(1)} %fusion.6), kind=kOutput, calls=%fused_computation.2 | convolution fusion | flops 2152202240 | bytes 10485760 | tf_op jit(solution)/shard_map/dot_general | solution.py:146
  78.3 2.0 %collective-permute-done.4 = bf16[128,2048]{1,0:T(8,128)(2,1)S(1)} collective-permute-done((bf16[128,2048]{1,0:T(8,128)(2,1)S(1)}, bf16[128,2048]{1,0:T(8,128)(2,1)S(1)}, u32[]{:S(2)}, u32[]{:S(2)}) %collective-permute-start.4) | collective-permute-done | bytes 524320 | tf_op jit(solution)/shard_map/ppermute | solution.py:16
  80.7 2.5 %collective-permute-start.7 = (bf16[64,2048]{1,0:T(8,128)(2,1)S(1)}, bf16[64,2048]{1,0:T(8,128)(2,1)S(1)}, u32[]{:S(2)}, u32[]{:S(2)}) collective-permute-start(bf16[64,2048]{1,0:T(8,128)(2,1)S(1)} %get-tuple-element.51), channel_id=1, source_target_pairs={{0,96},{32,0},{64,32},{96,64},{1,97},{33,1},{65,33},{97,65},{2,98}... | collective-permute-start | bytes 786440 | tf_op jit(solution)/shard_map/ppermute | solution.py:16
  83.5 2.7 %collective-permute-start.11 = (bf16[64,2048]{1,0:T(8,128)(2,1)S(1)}, bf16[64,2048]{1,0:T(8,128)(2,1)S(1)}, u32[]{:S(2)}, u32[]{:S(2)}) collective-permute-start(bf16[64,2048]{1,0:T(8,128)(2,1)S(1)} %slice.116), channel_id=1, source_target_pairs={{0,96},{32,0},{64,32},{96,64},{1,97},{33,1},{65,33},{97,65},{2,98}... | collective-permute-start | bytes 786440 | tf_op jit(solution)/shard_map/ppermute | solution.py:16
  86.6 3.1 %collective-permute-done.6 = bf16[64,2048]{1,0:T(8,128)(2,1)S(1)} collective-permute-done((bf16[64,2048]{1,0:T(8,128)(2,1)S(1)}, bf16[64,2048]{1,0:T(8,128)(2,1)S(1)}, u32[]{:S(2)}, u32[]{:S(2)}) %collective-permute-start.6) | collective-permute-done | bytes 262176 | tf_op jit(solution)/shard_map/ppermute | solution.py:16
  90.0 1.4 collective-permute-start.8
  91.5 2.8 %collective-permute-done.10 = bf16[64,2048]{1,0:T(8,128)(2,1)S(1)} collective-permute-done((bf16[64,2048]{1,0:T(8,128)(2,1)S(1)}, bf16[64,2048]{1,0:T(8,128)(2,1)S(1)}, u32[]{:S(2)}, u32[]{:S(2)}) %collective-permute-start.10) | collective-permute-done | bytes 262176 | tf_op jit(solution)/shard_map/ppermute | solution.py:16
  94.4 3.4 %fusion.21 = bf16[512,1024]{1,0:T(8,128)(2,1)S(1)} fusion(f32[512,1024]{1,0:T(8,128)S(1)} %fusion.6, bf16[512,2048]{1,0:T(8,128)(2,1)S(1)} %constant_dynamic-update-slice_fusion.5, bf16[1,1024,2048]{2,1,0:T(8,128)(2,1)S(1)} %copy-done.8), kind=kOutput, calls=%fused_computation.31 | convolution fusion | flops 2157969408 | bytes 9437184 | tf_op jit(solution)/shard_map/dot_general | solution.py:152
  97.8 2.4 %fusion.8 = bf16[512,2048]{1,0:T(8,128)(2,1)S(1)} fusion(bf16[512,1024]{1,0:T(8,128)(2,1)S(1)} %fusion.21, bf16[1,2048,1024]{2,1,0:T(8,128)(2,1)S(1)} %copy-done.9), kind=kOutput, calls=%fused_computation.12 | convolution fusion | flops 2148532224 | bytes 7340032 | tf_op jit(solution)/shard_map/dot_general | solution.py:154
  100.2 2.4 %collective-permute-done.9 = bf16[128,2048]{1,0:T(8,128)(2,1)S(1)} collective-permute-done((bf16[128,2048]{1,0:T(8,128)(2,1)S(1)}, bf16[128,2048]{1,0:T(8,128)(2,1)S(1)}, u32[]{:S(2)}, u32[]{:S(2)}) %collective-permute-start.9) | collective-permute-done | bytes 524320 | tf_op jit(solution)/shard_map/ppermute | solution.py:16
  102.7 2.8 %collective-permute-done.8 = bf16[128,2048]{1,0:T(8,128)(2,1)S(1)} collective-permute-done((bf16[128,2048]{1,0:T(8,128)(2,1)S(1)}, bf16[128,2048]{1,0:T(8,128)(2,1)S(1)}, u32[]{:S(2)}, u32[]{:S(2)}) %collective-permute-start.8) | collective-permute-done | bytes 524320 | tf_op jit(solution)/shard_map/ppermute | solution.py:16
  105.5 1.5 convolution_convert_fusion.1
  107.8 0.9 collective-permute-start.13
  108.8 11.4 %all-to-all-start.3 = ((bf16[32,8,2048]{2,1,0:T(8,128)(2,1)}), bf16[32,8,2048]{2,1,0:T(8,128)(2,1)S(1)}, u32[]{:S(2)}, u32[]{:S(2)}) async-start(bf16[32,8,2048]{2,1,0:T(8,128)(2,1)} %bitcast.11), calls=%async_computation.3 | async-start | bytes 2097152 | tf_op jit(solution)/shard_map/all_to_all | solution.py:66
  120.2 1.3 add_convert_fusion.2
  121.6 2.7 %collective-permute-start.15 = (bf16[64,2048]{1,0:T(8,128)(2,1)S(1)}, bf16[64,2048]{1,0:T(8,128)(2,1)S(1)}, u32[]{:S(2)}, u32[]{:S(2)}) collective-permute-start(bf16[64,2048]{1,0:T(8,128)(2,1)S(1)} %get-tuple-element.39), channel_id=1, source_target_pairs={{0,96},{32,0},{64,32},{96,64},{1,97},{33,1},{65,33},{97,65},{2,98}... | collective-permute-start | bytes 786440 | tf_op jit(solution)/shard_map/ppermute | solution.py:16
  124.3 4.1 %collective-permute-done.14 = bf16[64,2048]{1,0:T(8,128)(2,1)S(1)} collective-permute-done((bf16[64,2048]{1,0:T(8,128)(2,1)S(1)}, bf16[64,2048]{1,0:T(8,128)(2,1)S(1)}, u32[]{:S(2)}, u32[]{:S(2)}) %collective-permute-start.14) | collective-permute-done | bytes 262176 | tf_op jit(solution)/shard_map/ppermute | solution.py:16
  128.3 1.4 add_convert_fusion.1
  129.8 1.4 fusion.13
  131.2 6.1 %all-to-all-done.3 = bf16[32,8,2048]{2,1,0:T(8,128)(2,1)S(1)} async-done(((bf16[32,8,2048]{2,1,0:T(8,128)(2,1)}), bf16[32,8,2048]{2,1,0:T(8,128)(2,1)S(1)}, u32[]{:S(2)}, u32[]{:S(2)}) %all-to-all-start.3) | async-done | bytes 1048608 | tf_op jit(solution)/shard_map/all_to_all | solution.py:66
  137.4 5.2 %all-to-all-start.4 = ((bf16[32,8,2048]{2,1,0:T(8,128)(2,1)}), bf16[32,8,2048]{2,1,0:T(8,128)(2,1)S(1)}, u32[]{:S(2)}, u32[]{:S(2)}) async-start(bf16[32,8,2048]{2,1,0:T(8,128)(2,1)} %fusion.13), calls=%async_computation.4 | async-start | bytes 2097152 | tf_op jit(solution)/shard_map/all_to_all | solution.py:66
  142.6 6.4 %convert_bitcast_fusion.1 = bf16[1,2048,1024]{2,1,0:T(8,128)(2,1)} fusion(bf16[512,2048]{1,0:T(8,128)(2,1)} %constant_dynamic-update-slice_fusion, bf16[512,1024]{1,0:T(8,128)(2,1)} %copy-done.12), kind=kOutput, calls=%fused_computation.9 | convolution fusion | flops 2149580800 | bytes 7340032 | tf_op jit(solution)/shard_map/dot_general | solution.py:162
  149.0 4.6 %convert_bitcast_fusion = bf16[1,1024,2048]{2,1,0:T(8,128)(2,1)} fusion(bf16[512,2048]{1,0:T(8,128)(2,1)S(1)} %copy-done.6, f32[512,1024]{1,0:T(8,128)S(1)} %copy-done.11), kind=kOutput, calls=%fused_computation.8 | convolution fusion | flops 2154299392 | bytes 8388608 | tf_op jit(solution)/shard_map/dot_general | solution.py:165
  153.6 1.5 convolution_convert_fusion.3
  155.2 4.6 %all-to-all-done.4 = bf16[32,8,2048]{2,1,0:T(8,128)(2,1)S(1)} async-done(((bf16[32,8,2048]{2,1,0:T(8,128)(2,1)}), bf16[32,8,2048]{2,1,0:T(8,128)(2,1)S(1)}, u32[]{:S(2)}, u32[]{:S(2)}) %all-to-all-start.4) | async-done | bytes 1048608 | tf_op jit(solution)/shard_map/all_to_all | solution.py:66
  159.8 1.5 convolution_convert_fusion.2
  (63 shorter events, 3.8 us)
Async XLA Ops:
  0.6 19.1 %copy-start = (bf16[256,2048]{1,0:T(8,128)(2,1)S(1)}, bf16[256,2048]{1,0:T(8,128)(2,1)}, u32[]{:S(2)}) copy-start(bf16[256,2048]{1,0:T(8,128)(2,1)} %param.6) | copy-start | bytes 3145732
  0.6 0.7 copy-start.1
  2.3 17.2 %all-to-all-start = ((f32[32,8,128]{2,1,0:T(8,128)}), f32[32,8,128]{2,1,0:T(8,128)S(1)}, u32[]{:S(2)}, u32[]{:S(2)}) async-start(f32[32,8,128]{2,1,0:T(8,128)} %bitcast.1), calls=%async_computation | async-start | bytes 262144 | tf_op jit(solution)/shard_map/all_to_all | solution.py:66
  19.7 5.5 %copy-start.2 = (s32[1,1,128]{2,1,0:T(1,128)S(1)}, s32[1,1,128]{2,1,0:T(1,128)}, u32[]{:S(2)}) copy-start(s32[1,1,128]{2,1,0:T(1,128)} %param.8) | copy-start | bytes 1540
  19.7 5.7 %copy-start.4 = (bf16[256,2048]{1,0:T(8,128)(2,1)S(1)}, bf16[256,2048]{1,0:T(8,128)(2,1)}, u32[]{:S(2)}) copy-start(bf16[256,2048]{1,0:T(8,128)(2,1)} %param.7) | copy-start | bytes 3145732
  21.2 21.3 %all-to-all-start.1 = ((bf16[32,8,2048]{2,1,0:T(8,128)(2,1)}), bf16[32,8,2048]{2,1,0:T(8,128)(2,1)S(1)}, u32[]{:S(2)}, u32[]{:S(2)}) async-start(bf16[32,8,2048]{2,1,0:T(8,128)(2,1)} %fusion.12), calls=%async_computation.1 | async-start | bytes 2097152 | tf_op jit(solution)/shard_map/all_to_all | solution.py:66
  42.8 14.4 %collective-permute-start = (bf16[128,2048]{1,0:T(8,128)(2,1)S(1)}, bf16[128,2048]{1,0:T(8,128)(2,1)S(1)}, u32[]{:S(2)}, u32[]{:S(2)}) collective-permute-start(bf16[128,2048]{1,0:T(8,128)(2,1)S(1)} %convolution_convert_fusion.6), channel_id=1, source_target_pairs={{0,32},{32,64},{64,96},{96,0},{1,33},{33,65},{65,97},{97,1},{2,34}... | collective-permute-start | bytes 1572872 | tf_op jit(solution)/shard_map/ppermute | solution.py:16
  44.1 14.1 %collective-permute-start.1 = (bf16[128,2048]{1,0:T(8,128)(2,1)S(1)}, bf16[128,2048]{1,0:T(8,128)(2,1)}, u32[]{:S(2)}, u32[]{:S(2)}) collective-permute-start(bf16[128,2048]{1,0:T(8,128)(2,1)S(1)} %convolution_convert_fusion.6), channel_id=1, source_target_pairs={{0,96},{32,0},{64,32},{96,64},{1,97},{33,1},{65,33},{97,65},{2,98}... | collective-permute-start | bytes 1572872 | tf_op jit(solution)/shard_map/ppermute | solution.py:16
  45.6 21.8 %all-to-all-start.2 = ((bf16[32,8,2048]{2,1,0:T(8,128)(2,1)}), bf16[32,8,2048]{2,1,0:T(8,128)(2,1)S(1)}, u32[]{:S(2)}, u32[]{:S(2)}) async-start(bf16[32,8,2048]{2,1,0:T(8,128)(2,1)} %fusion.11), calls=%async_computation.2 | async-start | bytes 2097152 | tf_op jit(solution)/shard_map/all_to_all | solution.py:66
  58.0 9.4 %copy-start.7 = (f32[1,1,128]{2,1,0:T(1,128)S(1)}, f32[1,1,128]{2,1,0:T(1,128)}, u32[]{:S(2)}) copy-start(f32[1,1,128]{2,1,0:T(1,128)} %param.9) | copy-start | bytes 1540
  58.0 7.9 %collective-permute-start.2 = (bf16[64,2048]{1,0:T(8,128)(2,1)S(1)}, bf16[64,2048]{1,0:T(8,128)(2,1)S(1)}, u32[]{:S(2)}, u32[]{:S(2)}) collective-permute-start(bf16[64,2048]{1,0:T(8,128)(2,1)S(1)} %slice.109), channel_id=1, source_target_pairs={{0,32},{32,64},{64,96},{96,0},{1,33},{33,65},{65,97},{97,1},{2,34}... | collective-permute-start | bytes 786440 | tf_op jit(solution)/shard_map/ppermute | solution.py:16
  59.2 7.4 %collective-permute-start.3 = (bf16[64,2048]{1,0:T(8,128)(2,1)S(1)}, bf16[64,2048]{1,0:T(8,128)(2,1)S(1)}, u32[]{:S(2)}, u32[]{:S(2)}) collective-permute-start(bf16[64,2048]{1,0:T(8,128)(2,1)S(1)} %slice.110), channel_id=1, source_target_pairs={{0,96},{32,0},{64,32},{96,64},{1,97},{33,1},{65,33},{97,65},{2,98}... | collective-permute-start | bytes 786440 | tf_op jit(solution)/shard_map/ppermute | solution.py:16
  67.7 8.0 %copy-start.8 = (bf16[1,1024,2048]{2,1,0:T(8,128)(2,1)S(1)}, bf16[1,1024,2048]{2,1,0:T(8,128)(2,1)}, u32[]{:S(2)}) copy-start(bf16[1,1024,2048]{2,1,0:T(8,128)(2,1)} %param.11) | copy-start | bytes 12582916
  67.8 12.6 %collective-permute-start.4 = (bf16[128,2048]{1,0:T(8,128)(2,1)S(1)}, bf16[128,2048]{1,0:T(8,128)(2,1)S(1)}, u32[]{:S(2)}, u32[]{:S(2)}) collective-permute-start(bf16[128,2048]{1,0:T(8,128)(2,1)S(1)} %fusion.14), channel_id=1, source_target_pairs={{0,32},{32,64},{64,96},{96,0},{1,33},{33,65},{65,97},{97,1},{2,34}... | collective-permute-start | bytes 1572872 | tf_op jit(solution)/shard_map/ppermute | solution.py:16
  68.0 12.3 %collective-permute-start.5 = (bf16[128,2048]{1,0:T(8,128)(2,1)S(1)}, bf16[128,2048]{1,0:T(8,128)(2,1)S(1)}, u32[]{:S(2)}, u32[]{:S(2)}) collective-permute-start(bf16[128,2048]{1,0:T(8,128)(2,1)S(1)} %fusion.14), channel_id=1, source_target_pairs={{0,96},{32,0},{64,32},{96,64},{1,97},{33,1},{65,33},{97,65},{2,98}... | collective-permute-start | bytes 1572872 | tf_op jit(solution)/shard_map/ppermute | solution.py:16
  75.8 18.6 %copy-start.10 = (f32[512,1024]{1,0:T(8,128)}, f32[512,1024]{1,0:T(8,128)S(1)}, u32[]{:S(2)}) copy-start(f32[512,1024]{1,0:T(8,128)S(1)} %fusion.6) | copy-start | bytes 6291460
  80.7 5.9 %collective-permute-start.7 = (bf16[64,2048]{1,0:T(8,128)(2,1)S(1)}, bf16[64,2048]{1,0:T(8,128)(2,1)S(1)}, u32[]{:S(2)}, u32[]{:S(2)}) collective-permute-start(bf16[64,2048]{1,0:T(8,128)(2,1)S(1)} %get-tuple-element.51), channel_id=1, source_target_pairs={{0,96},{32,0},{64,32},{96,64},{1,97},{33,1},{65,33},{97,65},{2,98}... | collective-permute-start | bytes 786440 | tf_op jit(solution)/shard_map/ppermute | solution.py:16
  83.3 6.4 %collective-permute-start.6 = (bf16[64,2048]{1,0:T(8,128)(2,1)S(1)}, bf16[64,2048]{1,0:T(8,128)(2,1)S(1)}, u32[]{:S(2)}, u32[]{:S(2)}) collective-permute-start(bf16[64,2048]{1,0:T(8,128)(2,1)S(1)} %get-tuple-element.53), channel_id=1, source_target_pairs={{0,32},{32,64},{64,96},{96,0},{1,33},{33,65},{65,97},{97,1},{2,34}... | collective-permute-start | bytes 786440 | tf_op jit(solution)/shard_map/ppermute | solution.py:16
  83.3 10.9 %collective-permute-start.10 = (bf16[64,2048]{1,0:T(8,128)(2,1)S(1)}, bf16[64,2048]{1,0:T(8,128)(2,1)S(1)}, u32[]{:S(2)}, u32[]{:S(2)}) collective-permute-start(bf16[64,2048]{1,0:T(8,128)(2,1)S(1)} %slice.115), channel_id=1, source_target_pairs={{0,32},{32,64},{64,96},{96,0},{1,33},{33,65},{65,97},{97,1},{2,34}... | collective-permute-start | bytes 786440 | tf_op jit(solution)/shard_map/ppermute | solution.py:16
  83.5 10.8 %collective-permute-start.11 = (bf16[64,2048]{1,0:T(8,128)(2,1)S(1)}, bf16[64,2048]{1,0:T(8,128)(2,1)S(1)}, u32[]{:S(2)}, u32[]{:S(2)}) collective-permute-start(bf16[64,2048]{1,0:T(8,128)(2,1)S(1)} %slice.116), channel_id=1, source_target_pairs={{0,96},{32,0},{64,32},{96,64},{1,97},{33,1},{65,33},{97,65},{2,98}... | collective-permute-start | bytes 786440 | tf_op jit(solution)/shard_map/ppermute | solution.py:16
  89.9 12.7 %collective-permute-start.9 = (bf16[128,2048]{1,0:T(8,128)(2,1)S(1)}, bf16[128,2048]{1,0:T(8,128)(2,1)S(1)}, u32[]{:S(2)}, u32[]{:S(2)}) collective-permute-start(bf16[128,2048]{1,0:T(8,128)(2,1)S(1)} %get-tuple-element.32), channel_id=1, source_target_pairs={{0,96},{32,0},{64,32},{96,64},{1,97},{33,1},{65,33},{97,65},{2,98}... | collective-permute-start | bytes 1572872 | tf_op jit(solution)/shard_map/ppermute | solution.py:16
  90.0 15.5 %collective-permute-start.8 = (bf16[128,2048]{1,0:T(8,128)(2,1)S(1)}, bf16[128,2048]{1,0:T(8,128)(2,1)S(1)}, u32[]{:S(2)}, u32[]{:S(2)}) collective-permute-start(bf16[128,2048]{1,0:T(8,128)(2,1)S(1)} %get-tuple-element.31), channel_id=1, source_target_pairs={{0,32},{32,64},{64,96},{96,0},{1,33},{33,65},{65,97},{97,1},{2,34}... | collective-permute-start | bytes 1572872 | tf_op jit(solution)/shard_map/ppermute | solution.py:16
  94.3 3.5 %copy-start.5 = (bf16[512,2048]{1,0:T(8,128)(2,1)}, bf16[512,2048]{1,0:T(8,128)(2,1)S(1)}, u32[]{:S(2)}) copy-start(bf16[512,2048]{1,0:T(8,128)(2,1)S(1)} %constant_dynamic-update-slice_fusion.5) | copy-start | bytes 6291460
  94.3 3.5 %copy-start.9 = (bf16[1,2048,1024]{2,1,0:T(8,128)(2,1)S(1)}, bf16[1,2048,1024]{2,1,0:T(8,128)(2,1)}, u32[]{:S(2)}) copy-start(bf16[1,2048,1024]{2,1,0:T(8,128)(2,1)} %param.10) | copy-start | bytes 12582916
  97.8 2.4 %copy-start.12 = (bf16[512,1024]{1,0:T(8,128)(2,1)}, bf16[512,1024]{1,0:T(8,128)(2,1)S(1)}, u32[]{:S(2)}) copy-start(bf16[512,1024]{1,0:T(8,128)(2,1)S(1)} %fusion.21) | copy-start | bytes 3145732
  100.2 6.8 %copy-start.3 = (bf16[512,2048]{1,0:T(8,128)(2,1)}, bf16[512,2048]{1,0:T(8,128)(2,1)S(1)}, u32[]{:S(2)}) copy-start(bf16[512,2048]{1,0:T(8,128)(2,1)S(1)} %fusion.8) | copy-start | bytes 6291460
  107.1 13.1 %collective-permute-start.12 = (bf16[128,2048]{1,0:T(8,128)(2,1)S(1)}, bf16[128,2048]{1,0:T(8,128)(2,1)}, u32[]{:S(2)}, u32[]{:S(2)}) collective-permute-start(bf16[128,2048]{1,0:T(8,128)(2,1)S(1)} %pad_maximum_fusion.2), channel_id=1, source_target_pairs={{0,96},{32,0},{64,32},{96,64},{1,97},{33,1},{65,33},{97,65},{2,98}... | collective-permute-start | bytes 1572872 | tf_op jit(solution)/shard_map/ppermute | solution.py:16
  107.8 12.4 %collective-permute-start.13 = (bf16[128,2048]{1,0:T(8,128)(2,1)S(1)}, bf16[128,2048]{1,0:T(8,128)(2,1)}, u32[]{:S(2)}, u32[]{:S(2)}) collective-permute-start(bf16[128,2048]{1,0:T(8,128)(2,1)S(1)} %pad_maximum_fusion.3), channel_id=1, source_target_pairs={{0,32},{32,64},{64,96},{96,0},{1,33},{33,65},{65,97},{97,1},{2,34}... | collective-permute-start | bytes 1572872 | tf_op jit(solution)/shard_map/ppermute | solution.py:16
  108.8 28.6 %all-to-all-start.3 = ((bf16[32,8,2048]{2,1,0:T(8,128)(2,1)}), bf16[32,8,2048]{2,1,0:T(8,128)(2,1)S(1)}, u32[]{:S(2)}, u32[]{:S(2)}) async-start(bf16[32,8,2048]{2,1,0:T(8,128)(2,1)} %bitcast.11), calls=%async_computation.3 | async-start | bytes 2097152 | tf_op jit(solution)/shard_map/all_to_all | solution.py:66
  121.5 6.8 %collective-permute-start.14 = (bf16[64,2048]{1,0:T(8,128)(2,1)S(1)}, bf16[64,2048]{1,0:T(8,128)(2,1)S(1)}, u32[]{:S(2)}, u32[]{:S(2)}) collective-permute-start(bf16[64,2048]{1,0:T(8,128)(2,1)S(1)} %get-tuple-element.38), channel_id=1, source_target_pairs={{0,32},{32,64},{64,96},{96,0},{1,33},{33,65},{65,97},{97,1},{2,34}... | collective-permute-start | bytes 786440 | tf_op jit(solution)/shard_map/ppermute | solution.py:16
  121.6 6.7 %collective-permute-start.15 = (bf16[64,2048]{1,0:T(8,128)(2,1)S(1)}, bf16[64,2048]{1,0:T(8,128)(2,1)S(1)}, u32[]{:S(2)}, u32[]{:S(2)}) collective-permute-start(bf16[64,2048]{1,0:T(8,128)(2,1)S(1)} %get-tuple-element.39), channel_id=1, source_target_pairs={{0,96},{32,0},{64,32},{96,64},{1,97},{33,1},{65,33},{97,65},{2,98}... | collective-permute-start | bytes 786440 | tf_op jit(solution)/shard_map/ppermute | solution.py:16
  137.4 22.4 %all-to-all-start.4 = ((bf16[32,8,2048]{2,1,0:T(8,128)(2,1)}), bf16[32,8,2048]{2,1,0:T(8,128)(2,1)S(1)}, u32[]{:S(2)}, u32[]{:S(2)}) async-start(bf16[32,8,2048]{2,1,0:T(8,128)(2,1)} %fusion.13), calls=%async_computation.4 | async-start | bytes 2097152 | tf_op jit(solution)/shard_map/all_to_all | solution.py:66
  142.6 6.4 %copy-start.6 = (bf16[512,2048]{1,0:T(8,128)(2,1)S(1)}, bf16[512,2048]{1,0:T(8,128)(2,1)}, u32[]{:S(2)}) copy-start(bf16[512,2048]{1,0:T(8,128)(2,1)} %copy-done.5) | copy-start | bytes 6291460
  142.6 6.4 %copy-start.11 = (f32[512,1024]{1,0:T(8,128)S(1)}, f32[512,1024]{1,0:T(8,128)}, u32[]{:S(2)}) copy-start(f32[512,1024]{1,0:T(8,128)} %copy-done.10) | copy-start | bytes 6291460
